TPU v7x, 256 devices: a whole 4x4x8 slice. The times are simulated.
256 devices in a mesh: seq: 32 (over x_hi, z, core), head: 8 (over y, x_lo).
Axes of the slice: x: 4 (x_hi: 2, x_lo: 2; x = x_hi * 2 + x_lo), y: 4, z: 8, core: 2. Of those that a mesh axis runs over, the one named last changes fastest.
Arguments:
- query_rows: bfloat16 [16384, 8192], P('seq', 'head'), may hold values from -16 to 16
- key_rows: bfloat16 [16384, 1024], P('seq', 'head'), may hold values from -6 to 6
- value_rows: bfloat16 [16384, 1024], P('seq', 'head'), may hold values from -6 to 6
- out_grad: bfloat16 [16384, 8192], P('seq', 'head'), may hold values from -6 to 6
- random_blocks: int32 [128, 3], P('seq'), may hold values from 4 to 123, as said below
Outputs:
- attended: bfloat16 [16384, 8192], P('seq', 'head')
- query_grad: bfloat16 [16384, 8192], P('seq', 'head')
- key_grad: bfloat16 [16384, 1024], P('seq', 'head')
- value_grad: bfloat16 [16384, 1024], P('seq', 'head')
Inputs may be any that keep to these rules, and one draw needn't show every extreme that they name: `random_blocks`: every block named for a query block lies on another index of seq than the query block, than the two indices beside it, and than the first and the last index; the 3 blocks of one query block lie on 3 different indices. Over the rows of one index of seq, at most 1 named blocks lie on any one other index, and every index names exactly 1 block of some index. The rows of the blocks 0 and 127 are not read.
All inputs are finite; a program needn't handle non-finite values.
Results may differ from a plain program's by a relative error of at most 0.019.
Values may be sent and summed in bfloat16 or wider, within the bound.
No kernel may reach another device: no remote copies, remote signals or barrier semaphores. Data moves between devices by JAX's collectives and lax.ppermute only.
A program may use at most 192 MiB of HBM per device.

v0:
```python
import functools
import math

import jax
import jax.numpy as jnp
from jax import lax
from jax.experimental import pallas as pl
from jax.experimental.pallas import tpu as pltpu
from jax.sharding import PartitionSpec as P

D = 128
B = 128
SEQ = 32
ZN = 8
QB = 4
NB = SEQ * QB
HEADS = 8
ROWS = QB * B
PIECE = ROWS + 16
SLOTS = 8
KEYS = SLOTS * B
SCALE = 1.0 / math.sqrt(D)
LOG2E = math.log2(math.e)
FAR = -1e30
VMEM_LIMIT = 56 * 1024 * 1024
NT = (((1,), (1,)), ((), ()))
TN = (((0,), (0,)), ((), ()))


def device_of(x, z, c):
    return x * 16 + (z % ZN) * 2 + c


ALL = [(x, z, c) for x in range(2) for z in range(ZN) for c in range(2)]


CORE = [(i, i ^ 1) for i in range(SEQ)]
ACROSS = [(i, i ^ 16) for i in range(SEQ)]
Z_GROUPS = [[device_of(x, z, c) for z in range(ZN)] for x in range(2) for c in range(2)]
ZC_GROUPS = [[device_of(x, z, c) for z in range(ZN) for c in range(2)] for x in range(2)]
EDGE_Z = (0, ZN - 1)
EDGE_ACROSS = [(0, 16), (31, 15)]


def edge_tree(step):
    pairs = []
    for x in range(2):
        for c, sign in ((0, 1), (1, -1)):
            for r in range(0, ZN, 2 * step):
                ends = [EDGE_Z[c] + sign * r, EDGE_Z[c] + sign * (r + step)]
                pairs.append(tuple(device_of(x, z, c) for z in ends))
    return pairs


def to_edge(step):
    return [
        (device_of(x, EDGE_Z[c] + step, c), device_of(x, EDGE_Z[c], c))
        for x in range(2)
        for c in range(2)
    ]


def reverse(pairs):
    return [(b, a) for a, b in pairs]


def place_of(source, my_x):
    return ((source & 15) << 1) | ((source >> 4) ^ my_x)


def permute(value, pairs):
    return lax.ppermute(value, "seq", pairs)


def dot(a, b, dims=(((1,), (0,)), ((), ()))):
    return lax.dot_general(a, b, dims, preferred_element_type=jnp.float32)


def two_heads(ref_value, first):
    return jnp.concatenate(
        [ref_value[:, first : first + D], ref_value[:, first + D : first + 2 * D]], axis=0
    )


def edge_stats_kernel(edge_ref, k0, k1, k2, k3, stats_ref):
    stats_ref[...] = jnp.zeros_like(stats_ref)
    for pair in range(2):
        q2 = two_heads(edge_ref, pair * 2 * D)
        g2 = two_heads(edge_ref, 4 * D + pair * 2 * D)
        scores = [dot(k[:ROWS, :D], q2, NT) * (SCALE * LOG2E) for k in (k0, k1, k2, k3)]
        top = scores[0].max(axis=0, keepdims=True)
        for s in scores[1:]:
            top = jnp.maximum(top, s.max(axis=0, keepdims=True))
        total = jnp.zeros_like(top)
        delta = jnp.zeros_like(top)
        for s, k in zip(scores, (k0, k1, k2, k3)):
            e = jnp.exp2(s - top)
            total = total + e.sum(axis=0, keepdims=True)
            w = dot(k[:ROWS, D:], g2, NT)
            delta = delta + (e * w).sum(axis=0, keepdims=True)
        cols = slice(pair * 2 * D, (pair + 1) * 2 * D)
        stats_ref[0:1, cols] = top
        stats_ref[1:2, cols] = total
        stats_ref[2:3, cols] = delta


def edge_grad_kernel(
    edge_ref, k0, k1, k2, k3, stats_ref, oq_ref, own_ref, core_ref, across_ref
):
    stats = [stats_ref[n] for n in range(ZN)]
    top = stats[0][0:1]
    for s in stats[1:]:
        top = jnp.maximum(top, s[0:1])
    total = jnp.zeros_like(top)
    delta = jnp.zeros_like(top)
    for s in stats:
        factor = jnp.exp2(s[0:1] - top)
        total = total + s[1:2] * factor
        delta = delta + s[2:3] * factor
    delta = delta / total
    shift = top + jnp.log2(total)
    q_all = jnp.concatenate([two_heads(edge_ref, 0), two_heads(edge_ref, 2 * D)], axis=0)
    g_all = jnp.concatenate([two_heads(edge_ref, 4 * D), two_heads(edge_ref, 6 * D)], axis=0)
    out = None
    for n, k in enumerate((k0, k1, k2, k3)):
        keys = k[:ROWS, :D]
        values = k[:ROWS, D:]
        p = jnp.exp2(dot(keys, q_all, NT) * (SCALE * LOG2E) - shift)
        ds = (p * (dot(values, g_all, NT) - delta)).astype(jnp.bfloat16)
        p = p.astype(jnp.bfloat16)
        o = dot(values, p, TN)
        dq = dot(keys, ds, TN)
        out = (o, dq) if out is None else (out[0] + o, out[1] + dq)
        dk = dot(ds, q_all) * SCALE
        dv = dot(p, g_all)
        if n == 0:
            own_ref[:, :D] = dk
            own_ref[:, D:] = dv
        elif n == 1:
            across_ref[:, :D] = dk
            across_ref[:, D:] = dv
        else:
            core_ref[n - 2, :, :D] = dk.astype(jnp.bfloat16)
            core_ref[n - 2, :, D:] = dv.astype(jnp.bfloat16)
    for h in range(4):
        cols = slice(h * D, (h + 1) * D)
        oq_ref[:, cols] = out[0][:, cols].T.astype(jnp.bfloat16)
        oq_ref[:, 4 * D + h * D : 4 * D + (h + 1) * D] = (out[1][:, cols].T * SCALE).astype(
            jnp.bfloat16
        )


def middle_kernel(info, q_ref, g_ref, all_ref, _, *refs):
    out_ref, dq_ref, send_ref, state_ref, side_ref = refs[:5]
    kv, s_ref, e_all, ds_all, slots, sems, slot_sems = refs[5:]
    me = info[12]
    j = pl.program_id(0)
    last_step = j == QB - 1

    def fetch(block, buffer, slot):
        block = jnp.clip(block, 0, NB - 1)
        place = place_of(block >> 2, me >> 4)
        row = pl.multiple_of(place * PIECE + (block & 3) * B, 16)
        return pltpu.make_async_copy(
            all_ref.at[pl.ds(row, B), :], kv.at[buffer, pl.ds(slot * B, B), :], sems.at[buffer, slot]
        )

    def slot_copy(at, which, destination):
        return pltpu.make_async_copy(
            slots.at[at, which], send_ref.at[destination], slot_sems.at[at, which]
        )

    def fetch_all(step, buffer):
        block = me * QB + step
        for slot, name in enumerate((block - 1, block, block + 1, 0, NB - 1)):
            fetch(jnp.int32(name), buffer, slot).start()
        for r in range(3):
            fetch(info[step * 3 + r], buffer, 5 + r).start()

    @pl.when(j == 0)
    def _():
        fetch_all(0, 0)
        state_ref[...] = jnp.zeros_like(state_ref)
        side_ref[...] = jnp.zeros_like(side_ref)

    buffer = j & 1

    @pl.when(jnp.logical_not(last_step))
    def _():
        fetch_all(j + 1, 1 - buffer)

    for slot in range(SLOTS):
        fetch(jnp.int32(0), buffer, slot).wait()

    block = me * QB + j
    middle = jnp.logical_and(block > 0, block < NB - 1)
    to_low = jnp.logical_and(jnp.logical_and(middle, j == 0), me != 1)
    to_high = jnp.logical_and(jnp.logical_and(middle, j == QB - 1), me != SEQ - 2)

    @pl.when(middle)
    def _():
        low_bias = jnp.where(block == 1, FAR, 0.0).astype(jnp.float32)
        high_bias = jnp.where(block == NB - 2, FAR, 0.0).astype(jnp.float32)
        values_t = kv[buffer, :, D:].T
        keys_t = kv[buffer, :, :D].T
        scaled_q, scaled_g = [], []
        pairs = range(HEADS // 2)
        heads = [[slice((2 * p + h) * D, (2 * p + h + 1) * D) for h in range(2)] for p in pairs]
        chunks = [slice(n * B, (n + 1) * B) for n in range(KEYS // B)]

        def scores(pair):
            q_t = jnp.concatenate([q_ref[:, h].T for h in heads[pair]], axis=1)
            top = None
            for n, c in enumerate(chunks):
                s = dot(kv[buffer, c, :D], q_t)
                if n == 0:
                    s = s + low_bias
                if n == 2:
                    s = s + high_bias
                s_ref[pair % 2, c, :] = s
                m = s.max(axis=0, keepdims=True)
                top = m if top is None else jnp.maximum(top, m)
            return top * (SCALE * LOG2E)

        def weights(pair, top):
            cols = slice(pair * 2 * D, (pair + 1) * 2 * D)
            total = None
            for c in chunks:
                e = jnp.exp2(s_ref[pair % 2, c, :] * (SCALE * LOG2E) - top)
                e_all[c, cols] = e.astype(jnp.bfloat16)
                t = e.sum(axis=0, keepdims=True)
                total = t if total is None else total + t
            return 1.0 / total

        def gradients(pair, part):
            cols = slice(pair * 2 * D, (pair + 1) * 2 * D)
            g_t = jnp.concatenate([g_ref[:, h].T for h in heads[pair]], axis=1)
            o = dot(values_t, e_all[:, cols]) * part
            delta = (g_t.astype(jnp.float32) * o).sum(axis=0, keepdims=True)
            for c in chunks:
                e = e_all[c, cols].astype(jnp.float32)
                ds_all[c, cols] = (e * (dot(kv[buffer, c, D:], g_t) - delta)).astype(jnp.bfloat16)
            dq = dot(keys_t, ds_all[:, cols]) * (part * SCALE)
            for n, h in enumerate(heads[pair]):
                one = slice(n * B, (n + 1) * B)
                out_ref[:, h] = o[:, one].T.astype(jnp.bfloat16)
                dq_ref[:, h] = dq[:, one].T.astype(jnp.bfloat16)
                column = part[:, one].T
                scaled_q.append((q_ref[:, h] * (column * SCALE)).astype(jnp.bfloat16))
                scaled_g.append((g_ref[:, h] * column).astype(jnp.bfloat16))

        top = scores(0)
        for pair in pairs:
            part = weights(pair, top)
            if pair + 1 < HEADS // 2:
                top = scores(pair + 1)
            gradients(pair, part)
        dk = dot(ds_all[...], jnp.concatenate(scaled_q, axis=0))
        dv = dot(e_all[...], jnp.concatenate(scaled_g, axis=0))

        def contribution(slot):
            rows = slice(slot * B, (slot + 1) * B)
            return jnp.concatenate([dk[rows], dv[rows]], axis=1)

        def low(slot):
            return contribution(slot).astype(jnp.bfloat16)

        state_ref[pl.ds(pl.multiple_of(j * B, B), B), :] += contribution(1)
        state_ref[ROWS : ROWS + B, :] += contribution(3)
        state_ref[ROWS + B :, :] += contribution(4)

        @pl.when(j > 0)
        def _():
            state_ref[pl.ds(pl.multiple_of((j - 1) * B, B), B), :] += contribution(0)

        @pl.when(j < QB - 1)
        def _():
            state_ref[pl.ds(pl.multiple_of((j + 1) * B, B), B), :] += contribution(2)

        for r in range(3):
            slots[j, r] = low(5 + r)
            slot_copy(j, r, info[j * 3 + r] >> 2).start()

        @pl.when(j == 0)
        def _():
            slots[j, 3] = low(0)

        @pl.when(j == QB - 1)
        def _():
            slots[j, 3] = low(2)

        @pl.when(to_low)
        def _():
            slot_copy(j, 3, me - 1).start()

        @pl.when(to_high)
        def _():
            slot_copy(j, 3, me + 1).start()

        @pl.when(jnp.logical_and(j == 0, me == 1))
        def _():
            side_ref[...] = low(0)

        @pl.when(jnp.logical_and(j == QB - 1, me == SEQ - 2))
        def _():
            side_ref[...] = low(2)

    @pl.when(last_step)
    def _():
        slots[QB, 0] = state_ref[ROWS : ROWS + B, :].astype(jnp.bfloat16)
        slots[QB, 1] = state_ref[ROWS + B :, :].astype(jnp.bfloat16)

        @pl.when(me == 0)
        def _():
            state_ref[:B, :] += state_ref[ROWS : ROWS + B, :]

        @pl.when(me != 0)
        def _():
            slot_copy(QB, 0, 0).start()
            slot_copy(QB, 0, 0).wait()

        @pl.when(me == SEQ - 1)
        def _():
            state_ref[ROWS - B : ROWS, :] += state_ref[ROWS + B :, :]

        @pl.when(me != SEQ - 1)
        def _():
            slot_copy(QB, 1, SEQ - 1).start()
            slot_copy(QB, 1, SEQ - 1).wait()

    @pl.when(middle)
    def _():
        for r in range(3):
            slot_copy(j, r, 0).wait()

    @pl.when(jnp.logical_or(to_low, to_high))
    def _():
        slot_copy(j, 3, 0).wait()


def middle_call(info, query_rows, out_grad, gathered, later):
    bf16, f32 = jnp.bfloat16, jnp.float32
    anywhere = pl.BlockSpec(memory_space=pl.ANY)
    whole = pl.BlockSpec(memory_space=pltpu.VMEM)
    rows = pl.BlockSpec((B, HEADS * D), lambda j: (j, 0))
    return pl.pallas_call(
        middle_kernel,
        grid=(QB,),
        out_shape=[
            jax.ShapeDtypeStruct((ROWS, HEADS * D), bf16),
            jax.ShapeDtypeStruct((ROWS, HEADS * D), bf16),
            jax.ShapeDtypeStruct((SEQ, B, 2 * D), bf16),
            jax.ShapeDtypeStruct((ROWS + 2 * B, 2 * D), f32),
            jax.ShapeDtypeStruct((B, 2 * D), bf16),
        ],
        in_specs=[pl.BlockSpec(memory_space=pltpu.SMEM), rows, rows, anywhere, anywhere],
        out_specs=[rows, rows, anywhere, whole, whole],
        scratch_shapes=[
            pltpu.VMEM((2, KEYS, 2 * D), bf16),
            pltpu.VMEM((2, KEYS, 2 * D), f32),
            pltpu.VMEM((KEYS, HEADS * B), bf16),
            pltpu.VMEM((KEYS, HEADS * B), bf16),
            pltpu.VMEM((QB + 1, 4, B, 2 * D), bf16),
            pltpu.SemaphoreType.DMA((2, SLOTS)),
            pltpu.SemaphoreType.DMA((QB + 1, 4)),
        ],
        compiler_params=pltpu.CompilerParams(vmem_limit_bytes=VMEM_LIMIT),
        cost_estimate=pl.CostEstimate(
            flops=QB * 6 * 2 * KEYS * HEADS * B * D,
            bytes_accessed=QB * (4 << 20),
            transcendentals=QB * KEYS * HEADS * B,
        ),
    )(info, query_rows, out_grad, gathered, later)


def sum_kernel(
    target, recv_ref, extra_ref, own_ref, edge_ref, edge_core_ref, edge_across_ref, dk_ref, dv_ref, acc
):
    acc[...] = (
        own_ref[:ROWS, :]
        + edge_ref[...]
        + edge_core_ref[0].astype(jnp.float32)
        + edge_across_ref[...].astype(jnp.float32)
    )

    def add(s, carry):
        t = target[s]

        @pl.when(t >= 0)
        def _():
            rows = pl.ds(pl.multiple_of(t * B, B), B)
            acc[rows, :] += recv_ref[s].astype(jnp.float32)

        return carry

    lax.fori_loop(0, SEQ, add, 0)
    t = target[SEQ]

    @pl.when(t >= 0)
    def _():
        rows = pl.ds(pl.multiple_of(t * B, B), B)
        acc[rows, :] += extra_ref[...].astype(jnp.float32)

    dk_ref[...] = acc[:, :D].astype(jnp.bfloat16)
    dv_ref[...] = acc[:, D:].astype(jnp.bfloat16)


def call(kernel, outs, args, scalars=0, later=0, scratch=(), flops=0, bytes_accessed=0, exps=0):
    vmem = pl.BlockSpec(memory_space=pltpu.VMEM)
    smem = pl.BlockSpec(memory_space=pltpu.SMEM)
    return pl.pallas_call(
        kernel,
        out_shape=[jax.ShapeDtypeStruct(shape, dtype) for shape, dtype in outs],
        in_specs=[smem] * scalars
        + [vmem] * (len(args) - scalars - later)
        + [pl.BlockSpec(memory_space=pl.ANY)] * later,
        out_specs=[vmem] * len(outs),
        scratch_shapes=list(scratch),
        compiler_params=pltpu.CompilerParams(vmem_limit_bytes=VMEM_LIMIT),
        cost_estimate=pl.CostEstimate(
            flops=flops, bytes_accessed=bytes_accessed, transcendentals=exps
        ),
    )(*args)


def hold(*values):
    return lax.optimization_barrier(values)


def local(query_rows, key_rows, value_rows, out_grad, random_blocks):
    bf16, f32 = jnp.bfloat16, jnp.float32
    me = lax.axis_index("seq").astype(jnp.int32)
    my_x, my_z, my_c = me >> 4, (me >> 1) & 7, me & 1
    ids = random_blocks.reshape(QB * 3).astype(jnp.int32)

    at_edge = my_z == jnp.where(my_c == 0, EDGE_Z[0], EDGE_Z[1])
    is_root = jnp.logical_or(me == 0, me == SEQ - 1)
    edge_start = my_c * (ROWS - B)

    def edge_half(x):
        return jnp.concatenate(
            [
                lax.dynamic_slice(rows, (edge_start, x * (4 * D)), (B, 4 * D))
                for rows in (query_rows, out_grad)
            ],
            axis=1,
        )

    id_rows = jnp.zeros((PIECE - ROWS, 2 * D), bf16).at[0, : QB * 3].set(ids.astype(bf16))
    mine = jnp.concatenate([jnp.concatenate([key_rows, value_rows], axis=1), id_rows], axis=0)
    partner = permute(mine, ACROSS)
    near = [mine, partner, permute(mine, CORE), permute(partner, CORE)]

    edge = jnp.where(is_root, edge_half(my_x), permute(edge_half(1 - my_x), EDGE_ACROSS))
    edge = jnp.where(at_edge, edge, jnp.zeros_like(edge))
    edge = edge + permute(edge, edge_tree(4))
    both, edge = hold(jnp.concatenate([mine, partner], axis=0), edge)
    gathered = lax.all_gather(both, "seq", axis_index_groups=ZC_GROUPS, tiled=True)
    for step in (2, 1):
        edge = edge + permute(edge, edge_tree(step))

    edge_flops = 2 * 4 * ROWS * ROWS * D
    (stats,) = call(
        edge_stats_kernel,
        [((8, 4 * D), f32)],
        [edge] + near,
        flops=2 * edge_flops,
        bytes_accessed=2 << 20,
        exps=4 * ROWS * ROWS,
    )
    all_stats = lax.all_to_all(
        jnp.broadcast_to(stats, (ZN, *stats.shape)), "seq", 0, 0, axis_index_groups=Z_GROUPS
    )
    edge_oq, edge_own, edge_core, edge_across = call(
        edge_grad_kernel,
        [
            ((B, 8 * D), bf16),
            ((ROWS, 2 * D), f32),
            ((2, ROWS, 2 * D), bf16),
            ((ROWS, 2 * D), f32),
        ],
        [edge] + near + [all_stats],
        flops=6 * edge_flops,
        bytes_accessed=4 << 20,
        exps=4 * ROWS * ROWS,
    )
    edge_core = permute(edge_core, CORE)
    parts = [permute(edge_oq, to_edge(step)) for step in range(1, ZN)]
    edge_across = permute((edge_across + edge_core[1].astype(f32)).astype(bf16), ACROSS)

    info = jnp.concatenate([ids, me[None], jnp.zeros((3,), jnp.int32)])
    attended, query_grad, send, own, extra = middle_call(
        info, query_rows, out_grad, gathered, edge_oq
    )

    *parts, edge_across, send = hold(*parts, edge_across, send)
    oq_here = edge_oq.astype(f32)
    for part in parts:
        oq_here = oq_here + part.astype(f32)
    oq_here = oq_here.astype(bf16)
    oq_other = permute(oq_here, reverse(EDGE_ACROSS))
    extra = permute(extra, [(1, 0), (SEQ - 2, SEQ - 1)])
    recv = lax.all_to_all(send, "seq", 0, 0)

    table = gathered.reshape(SEQ, PIECE, 2 * D)[:, ROWS, : QB * 3].astype(jnp.int32)
    place = jnp.arange(SEQ, dtype=jnp.int32)
    source = (place >> 1) | (((place & 1) ^ my_x) << 4)
    row = source[:, None] * QB + jnp.arange(QB * 3, dtype=jnp.int32)[None, :] // 3
    read = jnp.logical_and(row > 0, row < NB - 1)
    mine_named = jnp.logical_and((table >> 2) == me, read)
    named = jnp.max(jnp.where(mine_named, table & 3, -1), axis=1)
    named = jnp.where(source == me - 1, 0, jnp.where(source == me + 1, QB - 1, named))
    named = jnp.where(me == 0, 0, jnp.where(me == SEQ - 1, QB - 1, named))
    named = jnp.where(source == me, -1, named)
    by_source = jnp.max(
        jnp.where(source[None, :] == place[:, None], named[None, :], -1), axis=1
    )
    extra_at = jnp.where(me == 0, QB - 1, jnp.where(me == SEQ - 1, 0, -1))
    target = jnp.concatenate([by_source, extra_at[None]]).astype(jnp.int32)

    key_grad, value_grad = call(
        sum_kernel,
        [((ROWS, D), bf16), ((ROWS, D), bf16)],
        [target, recv, extra, own, edge_own, edge_core, edge_across],
        scalars=1,
        scratch=[pltpu.VMEM((ROWS, 2 * D), f32)],
        flops=1 << 20,
        bytes_accessed=4 << 20,
    )

    low = jnp.where(my_x == 0, oq_here, oq_other)
    high = jnp.where(my_x == 0, oq_other, oq_here)

    def put(whole, start):
        edge_rows = jnp.concatenate(
            [low[:, start : start + 4 * D], high[:, start : start + 4 * D]], axis=1
        )
        present = lax.dynamic_slice(whole, (edge_start, 0), (B, HEADS * D))
        return lax.dynamic_update_slice(
            whole, jnp.where(is_root, edge_rows, present), (edge_start, 0)
        )

    return put(attended, 0), put(query_grad, 4 * D), key_grad, value_grad


def solution(mesh):
    rows = P("seq", "head")
    return jax.shard_map(
        local,
        mesh=mesh,
        in_specs=(rows, rows, rows, rows, P("seq", None)),
        out_specs=(rows, rows, rows, rows),
        check_vma=False,
    )
```

profile of v0, /device:TPU:1, one launch (start us, length us, event | category | flops | bytes accessed | tf_op | source)
XLA Modules:
  0.0 203.2 jit_solution(11947428097620658039)
XLA Ops:
  7.2 1.0 fusion.7
  8.2 1.0 fusion.8
  9.2 0.7 collective-permute-start.1
  9.9 0.9 constant_dynamic-update-slice_fusion.1
  10.9 0.7 convert_element_type.51
  11.6 0.9 constant_dynamic-update-slice_fusion
  12.6 3.7 %collective-permute-start = (bf16[528,256]{1,0:T(8,128)(2,1)S(1)}, bf16[528,256]{1,0:T(8,128)(2,1)S(1)}, u32[]{:S(2)}, u32[]{:S(2)}) collective-permute-start(bf16[528,256]{1,0:T(8,128)(2,1)S(1)} %pad_maximum_fusion.1.k0), channel_id=1, source_target_pairs={{0,128},{8,136},{16,144},{24,152},{32,160},{40,168},{48,176},{56,1... | collective-permute-start | bytes 811016 | tf_op jit(solution)/shard_map/ppermute | solution.py:72
  16.4 0.7 collective-permute-start.2
  17.1 5.4 %collective-permute-done.k1 = bf16[528,256]{1,0:T(8,128)(2,1)S(1)} collective-permute-done((bf16[528,256]{1,0:T(8,128)(2,1)S(1)}, bf16[528,256]{1,0:T(8,128)(2,1)S(1)}, u32[]{:S(2)}, u32[]{:S(2)}) %collective-permute-start) | collective-permute-done | bytes 270368 | tf_op jit(solution)/shard_map/ppermute | solution.py:72
  22.5 0.9 pad_maximum_fusion
  23.5 0.7 collective-permute-start.3
  24.2 7.6 %collective-permute-start.5 = (bf16[528,256]{1,0:T(8,128)(2,1)S(1)}, bf16[528,256]{1,0:T(8,128)(2,1)S(1)}, u32[]{:S(2)}, u32[]{:S(2)}) collective-permute-start(bf16[528,256]{1,0:T(8,128)(2,1)S(1)} %pad_maximum_fusion.1.k0), channel_id=1, source_target_pairs={{0,8},{8,0},{16,24},{24,16},{32,40},{40,32},{48,56},{56,48},{64,72... | collective-permute-start | bytes 811016 | tf_op jit(solution)/shard_map/ppermute | solution.py:72
  32.0 1.3 collective-permute-start.4
  33.3 9.9 %collective-permute-done.4 = bf16[128,1024]{1,0:T(8,128)(2,1)S(1)} collective-permute-done((bf16[128,1024]{1,0:T(8,128)(2,1)S(1)}, bf16[128,1024]{1,0:T(8,128)(2,1)S(1)}, u32[]{:S(2)}, u32[]{:S(2)}) %collective-permute-start.4) | collective-permute-done | bytes 262176 | tf_op jit(solution)/shard_map/ppermute | solution.py:72
  43.2 0.8 add.83.edge_ref
  44.0 0.7 copy-done.11
  44.7 0.7 copy-done.12
  45.4 3.9 %shard_map.84 = f32[8,512]{1,0:T(8,128)} custom-call(bf16[128,1024]{1,0:T(8,128)(2,1)} %add.83.edge_ref, bf16[528,256]{1,0:T(8,128)(2,1)} %copy-done.2, bf16[528,256]{1,0:T(8,128)(2,1)} %copy-done.3, bf16[528,256]{1,0:T(8,128)(2,1)} %copy-done.11, bf16[528,256]{1,0:T(8,128)(2,1)} %copy-done.12), custom_call_target="tpu_custom_call" | custom-call | flops 536870912 | bytes 2097152 | tf_op jit(solution)/shard_map/pallas_call | solution.py:411
  49.3 0.7 broadcast_in_dim.49
  50.0 12.5 %all_to_all.10.stats_ref = f32[8,8,512]{2,1,0:T(8,128)} all-to-all(f32[8,8,512]{2,1,0:T(8,128)S(1)} %broadcast_in_dim.49), channel_id=1, replica_groups={{0,16,32,48,64,80,96,112},{8,24,40,56,72,88,104,120},{128,144,160,176,1..., dimensions={0} | all-to-all | bytes 262144 | tf_op jit(solution)/shard_map/all_to_all | solution.py:471
  62.5 5.1 %shard_map.85 = (bf16[128,1024]{1,0:T(8,128)(2,1)}, f32[512,256]{1,0:T(8,128)}, bf16[2,512,256]{2,1,0:T(8,128)(2,1)}, f32[512,256]{1,0:T(8,128)}) custom-call(bf16[128,1024]{1,0:T(8,128)(2,1)} %add.83.edge_ref, bf16[528,256]{1,0:T(8,128)(2,1)} %copy-done.2, bf16[528,256]{1,0:T(8,128)(2,1)} %copy-done.3, bf16[528,256]{1,0:T(8,128)(2,1)} %copy-done.11, ...), custom_call_target="tpu_custom_call" | custom-call | flops 1610612736 | bytes 4194304 | tf_op jit(solution)/shard_map/pallas_call | solution.py:411
  67.7 9.6 %collective-permute-start.14 = (bf16[2,512,256]{2,1,0:T(8,128)(2,1)}, bf16[2,512,256]{2,1,0:T(8,128)(2,1)S(1)}, u32[]{:S(2)}, u32[]{:S(2)}) collective-permute-start(bf16[2,512,256]{2,1,0:T(8,128)(2,1)} %get-tuple-element.43), channel_id=1, source_target_pairs={{0,8},{8,0},{16,24},{24,16},{32,40},{40,32},{48,56},{56,48},{64,72... | collective-permute-start | bytes 1572872 | tf_op jit(solution)/shard_map/ppermute | solution.py:72
  77.3 0.7 collective-permute-start.13
  78.0 0.7 collective-permute-start.12
  78.7 1.4 collective-permute-start.11
  80.1 0.6 pad_add_fusion.info
  80.7 0.7 collective-permute-start.10
  81.3 0.7 collective-permute-start.9
  82.0 1.1 fusion
  83.2 0.7 collective-permute-start.8
  83.9 22.0 %collective-permute-start.7 = (bf16[128,1024]{1,0:T(8,128)(2,1)}, bf16[128,1024]{1,0:T(8,128)(2,1)S(1)}, u32[]{:S(2)}, u32[]{:S(2)}) collective-permute-start(bf16[128,1024]{1,0:T(8,128)(2,1)} %get-tuple-element.40._), channel_id=1, source_target_pairs={{16,0},{8,120},{144,128},{136,248},{17,1},{9,121},{145,129},{137,2... | collective-permute-start | bytes 786440 | tf_op jit(solution)/shard_map/ppermute | solution.py:72
  105.9 0.3 collective-permute-start.15
  106.2 23.7 %shard_map.86 = (bf16[512,1024]{1,0:T(8,128)(2,1)}, bf16[512,1024]{1,0:T(8,128)(2,1)}, bf16[32,128,256]{2,1,0:T(8,128)(2,1)}, f32[768,256]{1,0:T(8,128)}, bf16[128,256]{1,0:T(8,128)(2,1)}) custom-call(s32[16]{0:T(128)} %pad_add_fusion.info, bf16[512,1024]{1,0:T(8,128)(2,1)} %q_ref.1, bf16[512,1024]{1,0:T(8,128)(2,1)} %g_ref.1, ...), custom_call_target="tpu_custom_call" | custom-call | flops 6442450944 | bytes 16777216 | tf_op jit(solution)/shard_map/pallas_call | solution.py:346
  130.0 0.6 copy-done.6
  130.8 0.6 copy-done.4
  131.5 9.0 %all-to-all-start.1 = ((bf16[32,128,256]{2,1,0:T(8,128)(2,1)}), bf16[32,128,256]{2,1,0:T(8,128)(2,1)S(1)}, u32[]{:S(2)}, u32[]{:S(2)}) async-start(bf16[32,128,256]{2,1,0:T(8,128)(2,1)} %get-tuple-element.53), calls=%async_computation.1 | async-start | bytes 4194304 | tf_op jit(solution)/shard_map/all_to_all | solution.py:503
  140.5 2.1 %collective-permute-start.17 = (bf16[128,256]{1,0:T(8,128)(2,1)S(1)}, bf16[128,256]{1,0:T(8,128)(2,1)S(1)}, u32[]{:S(2)}, u32[]{:S(2)}) collective-permute-start(bf16[128,256]{1,0:T(8,128)(2,1)S(1)} %copy-done.13), channel_id=1, source_target_pairs={{8,0},{240,248},{9,1},{241,249},{10,2},{242,250},{11,3},{243,251},... | collective-permute-start | bytes 196616 | tf_op jit(solution)/shard_map/ppermute | solution.py:72
  142.6 1.5 add_convert_fusion
  144.2 0.7 collective-permute-start.16
  144.9 0.9 broadcast_and_fusion
  145.7 0.9 slice_convert_fusion
  146.6 0.2 select_reduce_fusion.1
  146.8 0.1 select_reduce_fusion
  146.9 0.7 pad_add_fusion.1.target
  147.7 2.0 fusion.2
  149.7 41.7 %all-to-all-done.1.recv_ref = bf16[32,128,256]{2,1,0:T(8,128)(2,1)S(1)} async-done(((bf16[32,128,256]{2,1,0:T(8,128)(2,1)}), bf16[32,128,256]{2,1,0:T(8,128)(2,1)S(1)}, u32[]{:S(2)}, u32[]{:S(2)}) %all-to-all-start.1) | async-done | bytes 2097184 | tf_op jit(solution)/shard_map/all_to_all | solution.py:503
  191.3 1.3 copy-done
  192.7 3.6 %shard_map.87 = (bf16[512,128]{1,0:T(8,128)(2,1)}, bf16[512,128]{1,0:T(8,128)(2,1)}) custom-call(s32[33]{0:T(128)} %pad_add_fusion.1.target, bf16[32,128,256]{2,1,0:T(8,128)(2,1)} %copy-done, bf16[128,256]{1,0:T(8,128)(2,1)} %copy-done.9, f32[768,256]{1,0:T(8,128)} %get-tuple-element.55.own_ref, f32[512,256]{1,0:T(8,128)} %get-tuple-element.56.edge_ref, ...), custom_call_target="tpu_custom_call" | custom-call | flops 1048576 | bytes 4194304 | tf_op jit(solution)/shard_map/pallas_call | solution.py:411
  (58 shorter events, 1.0 us)
Async XLA Ops:
  7.2 99.0 %all-gather.2.cloned.1.call-start = ((), (), s32[]{:S(2)}) async-start(), calls=%async_computation.2 | async-start | bytes 9191424 | tf_op jit(solution)/shard_map/all_gather | solution.py:458
  9.2 7.0 %collective-permute-start.1 = (bf16[128,1024]{1,0:T(8,128)(2,1)S(1)}, bf16[128,1024]{1,0:T(8,128)(2,1)S(1)}, u32[]{:S(2)}, u32[]{:S(2)}) collective-permute-start(bf16[128,1024]{1,0:T(8,128)(2,1)S(1)} %pad_maximum_fusion.2), channel_id=1, source_target_pairs={{0,128},{248,120},{1,129},{249,121},{2,130},{250,122},{3,131},{251... | collective-permute-start | bytes 786440 | tf_op jit(solution)/shard_map/ppermute | solution.py:72
  12.6 31.4 %copy-start.2 = (bf16[528,256]{1,0:T(8,128)(2,1)}, bf16[528,256]{1,0:T(8,128)(2,1)S(1)}, u32[]{:S(2)}) copy-start(bf16[528,256]{1,0:T(8,128)(2,1)S(1)} %pad_maximum_fusion.1.k0) | copy-start | bytes 811012
  12.6 9.9 %collective-permute-start = (bf16[528,256]{1,0:T(8,128)(2,1)S(1)}, bf16[528,256]{1,0:T(8,128)(2,1)S(1)}, u32[]{:S(2)}, u32[]{:S(2)}) collective-permute-start(bf16[528,256]{1,0:T(8,128)(2,1)S(1)} %pad_maximum_fusion.1.k0), channel_id=1, source_target_pairs={{0,128},{8,136},{16,144},{24,152},{32,160},{40,168},{48,176},{56,1... | collective-permute-start | bytes 811016 | tf_op jit(solution)/shard_map/ppermute | solution.py:72
  16.4 7.0 %collective-permute-start.2 = (bf16[128,1024]{1,0:T(8,128)(2,1)S(1)}, bf16[128,1024]{1,0:T(8,128)(2,1)S(1)}, u32[]{:S(2)}, u32[]{:S(2)}) collective-permute-start(bf16[128,1024]{1,0:T(8,128)(2,1)S(1)} %fusion.1), channel_id=1, source_target_pairs={{0,64},{120,56},{128,192},{248,184},{1,65},{121,57},{129,193},{249... | collective-permute-start | bytes 786440 | tf_op jit(solution)/shard_map/ppermute | solution.py:72
  22.5 21.5 %copy-start.3 = (bf16[528,256]{1,0:T(8,128)(2,1)}, bf16[528,256]{1,0:T(8,128)(2,1)S(1)}, u32[]{:S(2)}) copy-start(bf16[528,256]{1,0:T(8,128)(2,1)S(1)} %collective-permute-done.k1) | copy-start | bytes 811012
  23.5 8.4 %collective-permute-start.3 = (bf16[128,1024]{1,0:T(8,128)(2,1)S(1)}, bf16[128,1024]{1,0:T(8,128)(2,1)S(1)}, u32[]{:S(2)}, u32[]{:S(2)}) collective-permute-start(bf16[128,1024]{1,0:T(8,128)(2,1)S(1)} %add.81), channel_id=1, source_target_pairs={{0,32},{64,96},{120,88},{56,24},{128,160},{192,224},{248,216},{184... | collective-permute-start | bytes 786440 | tf_op jit(solution)/shard_map/ppermute | solution.py:72
  24.2 19.8 %collective-permute-start.5 = (bf16[528,256]{1,0:T(8,128)(2,1)S(1)}, bf16[528,256]{1,0:T(8,128)(2,1)S(1)}, u32[]{:S(2)}, u32[]{:S(2)}) collective-permute-start(bf16[528,256]{1,0:T(8,128)(2,1)S(1)} %pad_maximum_fusion.1.k0), channel_id=1, source_target_pairs={{0,8},{8,0},{16,24},{24,16},{32,40},{40,32},{48,56},{56,48},{64,72... | collective-permute-start | bytes 811016 | tf_op jit(solution)/shard_map/ppermute | solution.py:72
  31.8 12.2 %collective-permute-start.6 = (bf16[528,256]{1,0:T(8,128)(2,1)S(1)}, bf16[528,256]{1,0:T(8,128)(2,1)S(1)}, u32[]{:S(2)}, u32[]{:S(2)}) collective-permute-start(bf16[528,256]{1,0:T(8,128)(2,1)S(1)} %collective-permute-done.k1), channel_id=1, source_target_pairs={{0,8},{8,0},{16,24},{24,16},{32,40},{40,32},{48,56},{56,48},{64,72... | collective-permute-start | bytes 811016 | tf_op jit(solution)/shard_map/ppermute | solution.py:72
  32.0 11.2 %collective-permute-start.4 = (bf16[128,1024]{1,0:T(8,128)(2,1)S(1)}, bf16[128,1024]{1,0:T(8,128)(2,1)S(1)}, u32[]{:S(2)}, u32[]{:S(2)}) collective-permute-start(bf16[128,1024]{1,0:T(8,128)(2,1)S(1)} %add.82), channel_id=1, source_target_pairs={{0,16},{32,48},{64,80},{96,112},{120,104},{88,72},{56,40},{24,8},{... | collective-permute-start | bytes 786440 | tf_op jit(solution)/shard_map/ppermute | solution.py:72
  44.0 0.7 copy-start.11
  44.7 0.7 copy-start.12
  62.5 14.7 %copy-start.10 = (s32[4,3]{1,0:T(4,128)S(1)}, s32[4,3]{1,0:T(4,128)}, u32[]{:S(2)}) copy-start(s32[4,3]{1,0:T(4,128)} %param.11) | copy-start | bytes 148
  67.7 13.7 %collective-permute-start.14 = (bf16[2,512,256]{2,1,0:T(8,128)(2,1)}, bf16[2,512,256]{2,1,0:T(8,128)(2,1)S(1)}, u32[]{:S(2)}, u32[]{:S(2)}) collective-permute-start(bf16[2,512,256]{2,1,0:T(8,128)(2,1)} %get-tuple-element.43), channel_id=1, source_target_pairs={{0,8},{8,0},{16,24},{24,16},{32,40},{40,32},{48,56},{56,48},{64,72... | collective-permute-start | bytes 1572872 | tf_op jit(solution)/shard_map/ppermute | solution.py:72
  77.3 5.8 %collective-permute-start.13 = (bf16[128,1024]{1,0:T(8,128)(2,1)}, bf16[128,1024]{1,0:T(8,128)(2,1)S(1)}, u32[]{:S(2)}, u32[]{:S(2)}) collective-permute-start(bf16[128,1024]{1,0:T(8,128)(2,1)} %get-tuple-element.40._), channel_id=1, source_target_pairs={{112,0},{104,120},{240,128},{232,248},{113,1},{105,121},{241,129},... | collective-permute-start | bytes 786440 | tf_op jit(solution)/shard_map/ppermute | solution.py:72
  78.0 5.8 %collective-permute-start.12 = (bf16[128,1024]{1,0:T(8,128)(2,1)}, bf16[128,1024]{1,0:T(8,128)(2,1)S(1)}, u32[]{:S(2)}, u32[]{:S(2)}) collective-permute-start(bf16[128,1024]{1,0:T(8,128)(2,1)} %get-tuple-element.40._), channel_id=1, source_target_pairs={{96,0},{88,120},{224,128},{216,248},{97,1},{89,121},{225,129},{217... | collective-permute-start | bytes 786440 | tf_op jit(solution)/shard_map/ppermute | solution.py:72
  78.7 27.2 %collective-permute-start.11 = (bf16[128,1024]{1,0:T(8,128)(2,1)}, bf16[128,1024]{1,0:T(8,128)(2,1)}, u32[]{:S(2)}, u32[]{:S(2)}) collective-permute-start(bf16[128,1024]{1,0:T(8,128)(2,1)} %get-tuple-element.40._), channel_id=1, source_target_pairs={{80,0},{72,120},{208,128},{200,248},{81,1},{73,121},{209,129},{201... | collective-permute-start | bytes 786440 | tf_op jit(solution)/shard_map/ppermute | solution.py:72
  80.7 49.3 %collective-permute-start.10 = (bf16[128,1024]{1,0:T(8,128)(2,1)}, bf16[128,1024]{1,0:T(8,128)(2,1)S(1)}, u32[]{:S(2)}, u32[]{:S(2)}) collective-permute-start(bf16[128,1024]{1,0:T(8,128)(2,1)} %get-tuple-element.40._), channel_id=1, source_target_pairs={{64,0},{56,120},{192,128},{184,248},{65,1},{57,121},{193,129},{185... | collective-permute-start | bytes 786440 | tf_op jit(solution)/shard_map/ppermute | solution.py:72
  81.3 48.6 %copy-start.1 = (bf16[2,512,256]{2,1,0:T(8,128)(2,1)}, bf16[2,512,256]{2,1,0:T(8,128)(2,1)S(1)}, u32[]{:S(2)}) copy-start(bf16[2,512,256]{2,1,0:T(8,128)(2,1)S(1)} %collective-permute-done.14.edge_core_ref) | copy-start | bytes 1572868
  81.3 48.6 %collective-permute-start.9 = (bf16[128,1024]{1,0:T(8,128)(2,1)}, bf16[128,1024]{1,0:T(8,128)(2,1)S(1)}, u32[]{:S(2)}, u32[]{:S(2)}) collective-permute-start(bf16[128,1024]{1,0:T(8,128)(2,1)} %get-tuple-element.40._), channel_id=1, source_target_pairs={{48,0},{40,120},{176,128},{168,248},{49,1},{41,121},{177,129},{169... | collective-permute-start | bytes 786440 | tf_op jit(solution)/shard_map/ppermute | solution.py:72
  83.2 46.8 %collective-permute-start.8 = (bf16[128,1024]{1,0:T(8,128)(2,1)}, bf16[128,1024]{1,0:T(8,128)(2,1)S(1)}, u32[]{:S(2)}, u32[]{:S(2)}) collective-permute-start(bf16[128,1024]{1,0:T(8,128)(2,1)} %get-tuple-element.40._), channel_id=1, source_target_pairs={{32,0},{24,120},{160,128},{152,248},{33,1},{25,121},{161,129},{153... | collective-permute-start | bytes 786440 | tf_op jit(solution)/shard_map/ppermute | solution.py:72
  83.9 46.1 %collective-permute-start.7 = (bf16[128,1024]{1,0:T(8,128)(2,1)}, bf16[128,1024]{1,0:T(8,128)(2,1)S(1)}, u32[]{:S(2)}, u32[]{:S(2)}) collective-permute-start(bf16[128,1024]{1,0:T(8,128)(2,1)} %get-tuple-element.40._), channel_id=1, source_target_pairs={{16,0},{8,120},{144,128},{136,248},{17,1},{9,121},{145,129},{137,2... | collective-permute-start | bytes 786440 | tf_op jit(solution)/shard_map/ppermute | solution.py:72
  105.9 24.1 %collective-permute-start.15 = (bf16[512,256]{1,0:T(8,128)(2,1)S(1)}, bf16[512,256]{1,0:T(8,128)(2,1)S(1)}, u32[]{:S(2)}, u32[]{:S(2)}) collective-permute-start(bf16[512,256]{1,0:T(8,128)(2,1)S(1)} %fusion), channel_id=1, source_target_pairs={{0,128},{8,136},{16,144},{24,152},{32,160},{40,168},{48,176},{56,1... | collective-permute-start | bytes 786440 | tf_op jit(solution)/shard_map/ppermute | solution.py:72
  130.0 0.7 copy-start.6
  130.0 0.8 copy-start.7
  130.0 0.9 copy-start.8
  130.8 0.7 copy-start.4
  130.8 9.7 %copy-start.13 = (bf16[128,256]{1,0:T(8,128)(2,1)S(1)}, bf16[128,256]{1,0:T(8,128)(2,1)}, u32[]{:S(2)}) copy-start(bf16[128,256]{1,0:T(8,128)(2,1)} %get-tuple-element.54) | copy-start | bytes 196612
  130.8 11.9 %copy-start.5 = (bf16[128,1024]{1,0:T(8,128)(2,1)S(1)}, bf16[128,1024]{1,0:T(8,128)(2,1)}, u32[]{:S(2)}) copy-start(bf16[128,1024]{1,0:T(8,128)(2,1)} %get-tuple-element.40._) | copy-start | bytes 786436
  131.5 59.9 %all-to-all-start.1 = ((bf16[32,128,256]{2,1,0:T(8,128)(2,1)}), bf16[32,128,256]{2,1,0:T(8,128)(2,1)S(1)}, u32[]{:S(2)}, u32[]{:S(2)}) async-start(bf16[32,128,256]{2,1,0:T(8,128)(2,1)} %get-tuple-element.53), calls=%async_computation.1 | async-start | bytes 4194304 | tf_op jit(solution)/shard_map/all_to_all | solution.py:503
  140.5 9.2 %collective-permute-start.17 = (bf16[128,256]{1,0:T(8,128)(2,1)S(1)}, bf16[128,256]{1,0:T(8,128)(2,1)S(1)}, u32[]{:S(2)}, u32[]{:S(2)}) collective-permute-start(bf16[128,256]{1,0:T(8,128)(2,1)S(1)} %copy-done.13), channel_id=1, source_target_pairs={{8,0},{240,248},{9,1},{241,249},{10,2},{242,250},{11,3},{243,251},... | collective-permute-start | bytes 196616 | tf_op jit(solution)/shard_map/ppermute | solution.py:72
  144.2 3.4 %collective-permute-start.16 = (bf16[128,1024]{1,0:T(8,128)(2,1)S(1)}, bf16[128,1024]{1,0:T(8,128)(2,1)S(1)}, u32[]{:S(2)}, u32[]{:S(2)}) collective-permute-start(bf16[128,1024]{1,0:T(8,128)(2,1)S(1)} %add_convert_fusion), channel_id=1, source_target_pairs={{128,0},{120,248},{129,1},{121,249},{130,2},{122,250},{131,3},{123... | collective-permute-start | bytes 786440 | tf_op jit(solution)/shard_map/ppermute | solution.py:72
  149.7 41.7 %copy-start.9 = (bf16[128,256]{1,0:T(8,128)(2,1)}, bf16[128,256]{1,0:T(8,128)(2,1)S(1)}, u32[]{:S(2)}) copy-start(bf16[128,256]{1,0:T(8,128)(2,1)S(1)} %collective-permute-done.17.extra_ref) | copy-start | bytes 196612
  191.3 1.4 copy-start
Sparse Core Ops, SparseCore 0:
  23.6 81.7 all-gather.1
where the time goes:
time: 205 us; the launch traced here: 203 us
  starting transfers between devices  63.1 us (31%)
  waiting for transfers between devices  57.1 us (28%)
  Pallas kernels  36.4 us (18%)
  between operations  14.4 us (7%)
  blocking collectives  12.5 us (6%)
  other arithmetic  10.6 us (5%)
  local copies, waits for them, and re-layouts  9.03 us (4%)
    ppermute x18, starting transfers between devices, permute(): return lax.ppermute(value, 'seq', pairs)  54.1 us
    all_to_all x1, waiting for transfers between devices, local(): recv = lax.all_to_all(send, 'seq', 0, 0)  41.7 us
    pallas_call x1, Pallas kernels, middle_call(): pl.pallas_call(middle_kernel, grid=(QB,), out_shape=[jax.ShapeDtypeStruct...  23.7 us
    ppermute x18, waiting for transfers between devices, permute(): return lax.ppermute(value, 'seq', pairs)  15.4 us
    pallas_call x3, Pallas kernels, call(): pl.pallas_call(kernel, out_shape=[jax.ShapeDtypeStruct(shape, dtype) for...  12.6 us
    all_to_all x1, blocking collectives, local(): lax.all_to_all(jnp.broadcast_to(stats, (ZN, *stats.shape)), 'seq', 0, 0,...  12.5 us
    all_to_all x1, starting transfers between devices, local(): recv = lax.all_to_all(send, 'seq', 0, 0)  8.95 us
    unnamed x29, local copies, waits for them, and re-layouts  5.16 us
  transfers between devices with their start and end apart: 20, of which 3 were waited for; matrix products, arithmetic and copies ran while one was open for 7% of the time, Pallas kernels for 16%

commit v1 on v0

--- a/solution.py
+++ b/solution.py
@@ -42,6 +42,13 @@
 EDGE_ACROSS = [(0, 16), (31, 15)]
 
 
+def from_edge(step, across):
+    return [
+        (0, device_of(across, step, 0)),
+        (SEQ - 1, device_of(1 - across, ZN - 1 - step, 1)),
+    ]
+
+
 def edge_tree(step):
     pairs = []
     for x in range(2):
@@ -54,9 +61,9 @@
 
 def to_edge(step):
     return [
-        (device_of(x, EDGE_Z[c] + step, c), device_of(x, EDGE_Z[c], c))
+        (device_of(x, EDGE_Z[c] + sign * step, c), device_of(x, EDGE_Z[c], c))
         for x in range(2)
-        for c in range(2)
+        for c, sign in ((0, 1), (1, -1))
     ]
 
 
@@ -82,21 +89,83 @@
     )
 
 
-def edge_stats_kernel(edge_ref, k0, k1, k2, k3, stats_ref):
+def pack_kernel(ids_ref, k_ref, v_ref, mine_ref):
+    mine_ref[:ROWS, :D] = k_ref[...]
+    mine_ref[:ROWS, D:] = v_ref[...]
+    shape = (PIECE - ROWS, 2 * D)
+    column = lax.broadcasted_iota(jnp.int32, shape, 1)
+    ids = jnp.zeros(shape, jnp.int32)
+    for n in range(QB * 3):
+        ids = jnp.where(column == n, ids_ref[n // 3, n % 3], ids)
+    mine_ref[ROWS:, :] = ids.astype(jnp.float32).astype(jnp.bfloat16)
+
+
+def edge_kernel(info, q_ref, g_ref, _, own_ref, other_ref, sems):
+    me = info[12]
+    start = pl.multiple_of((me & 1) * (ROWS - B), B)
+    copies = []
+    for side, out in enumerate((own_ref, other_ref)):
+        first = pl.multiple_of(((me >> 4) ^ side) * (4 * D), D)
+        for n, rows in enumerate((q_ref, g_ref)):
+            copies.append(
+                pltpu.make_async_copy(
+                    rows.at[pl.ds(start, B), pl.ds(first, 4 * D)],
+                    out.at[:, pl.ds(n * 4 * D, 4 * D)],
+                    sems.at[side, n],
+                )
+            )
+    for copy in copies:
+        copy.start()
+    for copy in copies:
+        copy.wait()
+
+
+def put_kernel(info, low_ref, high_ref, out_in, dq_in, out_ref, dq_ref, sems):
+    me = info[12]
+    start = pl.multiple_of((me & 1) * (ROWS - B), B)
+    copies = []
+    for side, half in enumerate((low_ref, high_ref)):
+        for n, rows in enumerate((out_ref, dq_ref)):
+            copies.append(
+                pltpu.make_async_copy(
+                    half.at[:, pl.ds(n * 4 * D, 4 * D)],
+                    rows.at[pl.ds(start, B), pl.ds(side * 4 * D, 4 * D)],
+                    sems.at[side, n],
+                )
+            )
+
+    @pl.when(jnp.logical_or(me == 0, me == SEQ - 1))
+    def _():
+        for copy in copies:
+            copy.start()
+        for copy in copies:
+            copy.wait()
+
+
+def near_pieces(both_ref, core_ref):
+    return [
+        (ref[at : at + ROWS, :D], ref[at : at + ROWS, D:])
+        for ref in (both_ref, core_ref)
+        for at in (0, PIECE)
+    ]
+
+
+def edge_stats_kernel(edge_ref, both_ref, other_ref, stats_ref):
+    near = near_pieces(both_ref, other_ref)
     stats_ref[...] = jnp.zeros_like(stats_ref)
     for pair in range(2):
         q2 = two_heads(edge_ref, pair * 2 * D)
         g2 = two_heads(edge_ref, 4 * D + pair * 2 * D)
-        scores = [dot(k[:ROWS, :D], q2, NT) * (SCALE * LOG2E) for k in (k0, k1, k2, k3)]
+        scores = [dot(keys, q2, NT) * (SCALE * LOG2E) for keys, _ in near]
         top = scores[0].max(axis=0, keepdims=True)
         for s in scores[1:]:
             top = jnp.maximum(top, s.max(axis=0, keepdims=True))
         total = jnp.zeros_like(top)
         delta = jnp.zeros_like(top)
-        for s, k in zip(scores, (k0, k1, k2, k3)):
+        for s, (_, values) in zip(scores, near):
             e = jnp.exp2(s - top)
             total = total + e.sum(axis=0, keepdims=True)
-            w = dot(k[:ROWS, D:], g2, NT)
+            w = dot(values, g2, NT)
             delta = delta + (e * w).sum(axis=0, keepdims=True)
         cols = slice(pair * 2 * D, (pair + 1) * 2 * D)
         stats_ref[0:1, cols] = top
@@ -105,7 +174,7 @@
 
 
 def edge_grad_kernel(
-    edge_ref, k0, k1, k2, k3, stats_ref, oq_ref, own_ref, core_ref, across_ref
+    edge_ref, both_ref, other_ref, stats_ref, oq_ref, own_ref, core_ref, across_ref
 ):
     stats = [stats_ref[n] for n in range(ZN)]
     top = stats[0][0:1]
@@ -122,9 +191,7 @@
     q_all = jnp.concatenate([two_heads(edge_ref, 0), two_heads(edge_ref, 2 * D)], axis=0)
     g_all = jnp.concatenate([two_heads(edge_ref, 4 * D), two_heads(edge_ref, 6 * D)], axis=0)
     out = None
-    for n, k in enumerate((k0, k1, k2, k3)):
-        keys = k[:ROWS, :D]
-        values = k[:ROWS, D:]
+    for n, (keys, values) in enumerate(near_pieces(both_ref, other_ref)):
         p = jnp.exp2(dot(keys, q_all, NT) * (SCALE * LOG2E) - shift)
         ds = (p * (dot(values, g_all, NT) - delta)).astype(jnp.bfloat16)
         p = p.astype(jnp.bfloat16)
@@ -374,33 +441,55 @@
 
 
 def sum_kernel(
-    target, recv_ref, extra_ref, own_ref, edge_ref, edge_core_ref, edge_across_ref, dk_ref, dv_ref, acc
+    target,
+    extra_ref,
+    own_ref,
+    edge_ref,
+    edge_core_ref,
+    edge_across_ref,
+    recv_ref,
+    dk_ref,
+    dv_ref,
+    acc,
+    held,
+    sems,
 ):
+    def copy(s):
+        return pltpu.make_async_copy(recv_ref.at[s], held.at[s], sems.at[s])
+
+    def begin(s, carry):
+        @pl.when(target[s] >= 0)
+        def _():
+            copy(s).start()
+
+        return carry
+
+    lax.fori_loop(0, SEQ, begin, 0)
     acc[...] = (
         own_ref[:ROWS, :]
         + edge_ref[...]
         + edge_core_ref[0].astype(jnp.float32)
         + edge_across_ref[...].astype(jnp.float32)
     )
+    t = target[SEQ]
+
+    @pl.when(t >= 0)
+    def _():
+        rows = pl.ds(pl.multiple_of(t * B, B), B)
+        acc[rows, :] += extra_ref[...].astype(jnp.float32)
 
     def add(s, carry):
         t = target[s]
 
         @pl.when(t >= 0)
         def _():
+            copy(s).wait()
             rows = pl.ds(pl.multiple_of(t * B, B), B)
-            acc[rows, :] += recv_ref[s].astype(jnp.float32)
+            acc[rows, :] += held[s].astype(jnp.float32)
 
         return carry
 
     lax.fori_loop(0, SEQ, add, 0)
-    t = target[SEQ]
-
-    @pl.when(t >= 0)
-    def _():
-        rows = pl.ds(pl.multiple_of(t * B, B), B)
-        acc[rows, :] += extra_ref[...].astype(jnp.float32)
-
     dk_ref[...] = acc[:, :D].astype(jnp.bfloat16)
     dv_ref[...] = acc[:, D:].astype(jnp.bfloat16)
 
@@ -433,29 +522,35 @@
     my_x, my_z, my_c = me >> 4, (me >> 1) & 7, me & 1
     ids = random_blocks.reshape(QB * 3).astype(jnp.int32)
 
-    at_edge = my_z == jnp.where(my_c == 0, EDGE_Z[0], EDGE_Z[1])
     is_root = jnp.logical_or(me == 0, me == SEQ - 1)
-    edge_start = my_c * (ROWS - B)
-
-    def edge_half(x):
-        return jnp.concatenate(
-            [
-                lax.dynamic_slice(rows, (edge_start, x * (4 * D)), (B, 4 * D))
-                for rows in (query_rows, out_grad)
-            ],
-            axis=1,
-        )
-
-    id_rows = jnp.zeros((PIECE - ROWS, 2 * D), bf16).at[0, : QB * 3].set(ids.astype(bf16))
-    mine = jnp.concatenate([jnp.concatenate([key_rows, value_rows], axis=1), id_rows], axis=0)
+    info = jnp.concatenate([ids, me[None], jnp.zeros((3,), jnp.int32)])
+    smem = pl.BlockSpec(memory_space=pltpu.SMEM)
+    vmem = pl.BlockSpec(memory_space=pltpu.VMEM)
+    anywhere = pl.BlockSpec(memory_space=pl.ANY)
+    (mine,) = call(
+        pack_kernel,
+        [((PIECE, 2 * D), bf16)],
+        [random_blocks, key_rows, value_rows],
+        scalars=1,
+        bytes_accessed=1 << 19,
+    )
     partner = permute(mine, ACROSS)
-    near = [mine, partner, permute(mine, CORE), permute(partner, CORE)]
-
-    edge = jnp.where(is_root, edge_half(my_x), permute(edge_half(1 - my_x), EDGE_ACROSS))
-    edge = jnp.where(at_edge, edge, jnp.zeros_like(edge))
-    edge = edge + permute(edge, edge_tree(4))
+    edge_own, edge_other = pl.pallas_call(
+        edge_kernel,
+        out_shape=[jax.ShapeDtypeStruct((B, 8 * D), bf16)] * 2,
+        in_specs=[smem, anywhere, anywhere, anywhere],
+        out_specs=[vmem, vmem],
+        scratch_shapes=[pltpu.SemaphoreType.DMA((2, 2))],
+        cost_estimate=pl.CostEstimate(flops=0, bytes_accessed=1 << 27, transcendentals=0),
+    )(info, query_rows, out_grad, mine)
+
+    edge = jnp.where(is_root, edge_own, jnp.zeros_like(edge_own))
+    edge = edge + permute(edge_other, from_edge(0, 1))
+    edge = edge + permute(edge_own, from_edge(4, 0))
+    edge = edge + permute(edge_other, from_edge(4, 1))
     both, edge = hold(jnp.concatenate([mine, partner], axis=0), edge)
     gathered = lax.all_gather(both, "seq", axis_index_groups=ZC_GROUPS, tiled=True)
+    near = [both, permute(both, CORE)]
     for step in (2, 1):
         edge = edge + permute(edge, edge_tree(step))
 
@@ -471,7 +566,7 @@
     all_stats = lax.all_to_all(
         jnp.broadcast_to(stats, (ZN, *stats.shape)), "seq", 0, 0, axis_index_groups=Z_GROUPS
     )
-    edge_oq, edge_own, edge_core, edge_across = call(
+    edge_oq, edge_mine, edge_core, edge_across = call(
         edge_grad_kernel,
         [
             ((B, 8 * D), bf16),
@@ -485,19 +580,20 @@
         exps=4 * ROWS * ROWS,
     )
     edge_core = permute(edge_core, CORE)
-    parts = [permute(edge_oq, to_edge(step)) for step in range(1, ZN)]
+    oq_sum = edge_oq.astype(f32)
+    oq_sum = oq_sum + permute(edge_oq, reverse(edge_tree(1))).astype(f32)
+    oq_low = oq_sum.astype(bf16)
+    oq_far = [permute(oq_low, to_edge(step)) for step in (4, 6, 2)]
     edge_across = permute((edge_across + edge_core[1].astype(f32)).astype(bf16), ACROSS)
 
-    info = jnp.concatenate([ids, me[None], jnp.zeros((3,), jnp.int32)])
     attended, query_grad, send, own, extra = middle_call(
-        info, query_rows, out_grad, gathered, edge_oq
-    )
-
-    *parts, edge_across, send = hold(*parts, edge_across, send)
-    oq_here = edge_oq.astype(f32)
-    for part in parts:
-        oq_here = oq_here + part.astype(f32)
-    oq_here = oq_here.astype(bf16)
+        info, query_rows, out_grad, gathered, oq_low
+    )
+
+    *oq_far, edge_across, send = hold(*oq_far, edge_across, send)
+    for part in oq_far:
+        oq_sum = oq_sum + part.astype(f32)
+    oq_here = oq_sum.astype(bf16)
     oq_other = permute(oq_here, reverse(EDGE_ACROSS))
     extra = permute(extra, [(1, 0), (SEQ - 2, SEQ - 1)])
     recv = lax.all_to_all(send, "seq", 0, 0)
@@ -521,9 +617,14 @@
     key_grad, value_grad = call(
         sum_kernel,
         [((ROWS, D), bf16), ((ROWS, D), bf16)],
-        [target, recv, extra, own, edge_own, edge_core, edge_across],
+        [target, extra, own, edge_mine, edge_core, edge_across, recv],
         scalars=1,
-        scratch=[pltpu.VMEM((ROWS, 2 * D), f32)],
+        later=1,
+        scratch=[
+            pltpu.VMEM((ROWS, 2 * D), f32),
+            pltpu.VMEM((SEQ, B, 2 * D), bf16),
+            pltpu.SemaphoreType.DMA((SEQ,)),
+        ],
         flops=1 << 20,
         bytes_accessed=4 << 20,
     )
@@ -531,16 +632,17 @@
     low = jnp.where(my_x == 0, oq_here, oq_other)
     high = jnp.where(my_x == 0, oq_other, oq_here)
 
-    def put(whole, start):
-        edge_rows = jnp.concatenate(
-            [low[:, start : start + 4 * D], high[:, start : start + 4 * D]], axis=1
-        )
-        present = lax.dynamic_slice(whole, (edge_start, 0), (B, HEADS * D))
-        return lax.dynamic_update_slice(
-            whole, jnp.where(is_root, edge_rows, present), (edge_start, 0)
-        )
-
-    return put(attended, 0), put(query_grad, 4 * D), key_grad, value_grad
+    rows = jax.ShapeDtypeStruct((ROWS, HEADS * D), bf16)
+    attended, query_grad = pl.pallas_call(
+        put_kernel,
+        out_shape=[rows, rows],
+        in_specs=[smem, vmem, vmem, anywhere, anywhere],
+        out_specs=[anywhere, anywhere],
+        input_output_aliases={3: 0, 4: 1},
+        scratch_shapes=[pltpu.SemaphoreType.DMA((2, 2))],
+        cost_estimate=pl.CostEstimate(flops=0, bytes_accessed=1 << 20, transcendentals=0),
+    )(info, low, high, attended, query_grad)
+    return attended, query_grad, key_grad, value_grad
 
 
 def solution(mesh):

time: 205 us -> 201 us (0.980)
  starting transfers between devices: 63.1 us -> 52.3 us
  Pallas kernels: 36.4 us -> 42.2 us
  waiting for transfers between devices: 57.1 us -> 62.2 us
  local copies, waits for them, and re-layouts: 9.03 us -> 5.05 us
    ppermute x18 -> x15, starting transfers between devices: 54.1 us -> 41.1 us  [permute(): return lax.ppermute(value, 'seq', pairs)]
    ppermute x18 -> x15, waiting for transfers between devices: 15.4 us -> 20 us  [permute(): return lax.ppermute(value, 'seq', pairs)]
    pallas_call x0 -> x2, Pallas kernels: none -> 3.67 us  [the longest x1 2.58 us: local(): pl.pallas_call(edge_kernel, out_shape=[jax.ShapeDtypeStruct((B, 8 * D), b...]
    pallas_call x3 -> x4, Pallas kernels: 12.6 us -> 14.8 us  [call(): pl.pallas_call(kernel, out_shape=[jax.ShapeDtypeStruct(shape, dtype) for...]
    all_to_all x1, starting transfers between devices: 8.95 us -> 11.1 us  [local(): recv = lax.all_to_all(send, 'seq', 0, 0)]
    unnamed x29 -> x20, local copies, waits for them, and re-layouts: 5.16 us -> 3.56 us
  transfers between devices with their start and end apart: 20 -> 17, of which waited for: 3 -> 4; matrix products, arithmetic and copies ran while one was open for 7% -> 4% of each run, Pallas kernels for 16% -> 17%
where the time goes in v1:
time: 201 us; the launch traced here: 199 us
  waiting for transfers between devices  62.2 us (31%)
  starting transfers between devices  52.3 us (26%)
  Pallas kernels  42.2 us (21%)
  between operations  14.4 us (7%)
  blocking collectives  13.9 us (7%)
  other arithmetic  9.37 us (5%)
  local copies, waits for them, and re-layouts  5.05 us (3%)
    all_to_all x1, waiting for transfers between devices, local(): recv = lax.all_to_all(send, 'seq', 0, 0)  42.2 us
    ppermute x15, starting transfers between devices, permute(): return lax.ppermute(value, 'seq', pairs)  41.1 us
    pallas_call x1, Pallas kernels, middle_call(): pl.pallas_call(middle_kernel, grid=(QB,), out_shape=[jax.ShapeDtypeStruct...  23.7 us
    ppermute x15, waiting for transfers between devices, permute(): return lax.ppermute(value, 'seq', pairs)  20 us
    pallas_call x4, Pallas kernels, call(): pl.pallas_call(kernel, out_shape=[jax.ShapeDtypeStruct(shape, dtype) for...  14.8 us
    all_to_all x1, blocking collectives, local(): lax.all_to_all(jnp.broadcast_to(stats, (ZN, *stats.shape)), 'seq', 0, 0,...  13.9 us
    all_to_all x1, starting transfers between devices, local(): recv = lax.all_to_all(send, 'seq', 0, 0)  11.1 us
  transfers between devices with their start and end apart: 17, of which 4 were waited for; matrix products, arithmetic and copies ran while one was open for 4% of the time, Pallas kernels for 17%

profile of v1, /device:TPU:1, one launch (start us, length us, event | category | flops | bytes accessed | tf_op | source)
XLA Modules:
  0.0 199.4 jit_solution(7331315845091219621)
XLA Ops:
  7.2 0.8 reshape.78
  8.0 1.7 shard_map.84._
  9.7 0.6 pad_add_fusion.info
  10.3 2.6 %shard_map.85 = (bf16[128,1024]{1,0:T(8,128)(2,1)}, bf16[128,1024]{1,0:T(8,128)(2,1)}) custom-call(s32[16]{0:T(128)} %pad_add_fusion.info, bf16[512,1024]{1,0:T(8,128)(2,1)} %q_ref.3, bf16[512,1024]{1,0:T(8,128)(2,1)} %g_ref.3, bf16[528,256]{1,0:T(8,128)(2,1)} %shard_map.84._), custom_call_target="tpu_custom_call" | custom-call | bytes 134217728 | tf_op jit(solution)/shard_map/pallas_call | solution.py:538
  12.9 0.7 collective-permute-start.2
  13.6 0.7 collective-permute-start.3
  14.3 0.7 collective-permute-start.1
  15.0 3.7 %collective-permute-start = (bf16[528,256]{1,0:T(8,128)(2,1)S(1)}, bf16[528,256]{1,0:T(8,128)(2,1)S(1)}, u32[]{:S(2)}, u32[]{:S(2)}) collective-permute-start(bf16[528,256]{1,0:T(8,128)(2,1)S(1)} %copy-done.1), channel_id=1, source_target_pairs={{0,128},{8,136},{16,144},{24,152},{32,160},{40,168},{48,176},{56,1... | collective-permute-start | bytes 811016 | tf_op jit(solution)/shard_map/ppermute | solution.py:79
  18.7 0.1 add_add_fusion
  18.7 3.8 %collective-permute-done = bf16[528,256]{1,0:T(8,128)(2,1)S(1)} collective-permute-done((bf16[528,256]{1,0:T(8,128)(2,1)S(1)}, bf16[528,256]{1,0:T(8,128)(2,1)S(1)}, u32[]{:S(2)}, u32[]{:S(2)}) %collective-permute-start) | collective-permute-done | bytes 270368 | tf_op jit(solution)/shard_map/ppermute | solution.py:79
  22.5 0.8 pad_maximum_fusion.both_ref
  23.3 13.7 %collective-permute-start.6 = (bf16[1056,256]{1,0:T(8,128)(2,1)}, bf16[1056,256]{1,0:T(8,128)(2,1)S(1)}, u32[]{:S(2)}, u32[]{:S(2)}) collective-permute-start(bf16[1056,256]{1,0:T(8,128)(2,1)} %pad_maximum_fusion.both_ref), channel_id=1, source_target_pairs={{0,8},{8,0},{16,24},{24,16},{32,40},{40,32},{48,56},{56,48},{64,72... | collective-permute-start | bytes 1622024 | tf_op jit(solution)/shard_map/ppermute | solution.py:79
  37.0 0.7 collective-permute-start.4
  37.7 0.1 add.56
  37.8 1.3 collective-permute-start.5
  39.1 7.0 %collective-permute-done.5 = bf16[128,1024]{1,0:T(8,128)(2,1)S(1)} collective-permute-done((bf16[128,1024]{1,0:T(8,128)(2,1)S(1)}, bf16[128,1024]{1,0:T(8,128)(2,1)S(1)}, u32[]{:S(2)}, u32[]{:S(2)}) %collective-permute-start.5) | collective-permute-done | bytes 262176 | tf_op jit(solution)/shard_map/ppermute | solution.py:79
  46.1 0.8 add.57.edge_ref
  46.8 0.8 copy-done.8
  47.6 3.8 %shard_map.86 = f32[8,512]{1,0:T(8,128)} custom-call(bf16[128,1024]{1,0:T(8,128)(2,1)} %add.57.edge_ref, bf16[1056,256]{1,0:T(8,128)(2,1)} %pad_maximum_fusion.both_ref, bf16[1056,256]{1,0:T(8,128)(2,1)} %copy-done.8), custom_call_target="tpu_custom_call" | custom-call | flops 536870912 | bytes 2097152 | tf_op jit(solution)/shard_map/pallas_call | solution.py:500
  51.4 0.7 broadcast_in_dim.48
  52.2 13.9 %all_to_all.10.stats_ref = f32[8,8,512]{2,1,0:T(8,128)} all-to-all(f32[8,8,512]{2,1,0:T(8,128)S(1)} %broadcast_in_dim.48), channel_id=1, replica_groups={{0,16,32,48,64,80,96,112},{8,24,40,56,72,88,104,120},{128,144,160,176,1..., dimensions={0} | all-to-all | bytes 262144 | tf_op jit(solution)/shard_map/all_to_all | solution.py:566
  66.1 5.2 %shard_map.87 = (bf16[128,1024]{1,0:T(8,128)(2,1)}, f32[512,256]{1,0:T(8,128)}, bf16[2,512,256]{2,1,0:T(8,128)(2,1)}, f32[512,256]{1,0:T(8,128)}) custom-call(bf16[128,1024]{1,0:T(8,128)(2,1)} %add.57.edge_ref, bf16[1056,256]{1,0:T(8,128)(2,1)} %pad_maximum_fusion.both_ref, bf16[1056,256]{1,0:T(8,128)(2,1)} %copy-done.8, f32[8,8,512]{2,1,0:T(8,128)} %all_to_all.10.stats_ref), custom_call_target="tpu_custom_call" | custom-call | flops 1610612736 | bytes 4194304 | tf_op jit(solution)/shard_map/pallas_call | solution.py:500
  71.4 9.8 %collective-permute-start.11 = (bf16[2,512,256]{2,1,0:T(8,128)(2,1)}, bf16[2,512,256]{2,1,0:T(8,128)(2,1)S(1)}, u32[]{:S(2)}, u32[]{:S(2)}) collective-permute-start(bf16[2,512,256]{2,1,0:T(8,128)(2,1)} %get-tuple-element.32), channel_id=1, source_target_pairs={{0,8},{8,0},{16,24},{24,16},{32,40},{40,32},{48,56},{56,48},{64,72... | collective-permute-start | bytes 1572872 | tf_op jit(solution)/shard_map/ppermute | solution.py:79
  81.2 2.2 %collective-permute-start.7 = (bf16[128,1024]{1,0:T(8,128)(2,1)}, bf16[128,1024]{1,0:T(8,128)(2,1)S(1)}, u32[]{:S(2)}, u32[]{:S(2)}) collective-permute-start(bf16[128,1024]{1,0:T(8,128)(2,1)} %get-tuple-element.30), channel_id=1, source_target_pairs={{16,0},{48,32},{80,64},{112,96},{104,120},{72,88},{40,56},{8,24},{... | collective-permute-start | bytes 786440 | tf_op jit(solution)/shard_map/ppermute | solution.py:79
  83.4 9.2 %collective-permute-done.7 = bf16[128,1024]{1,0:T(8,128)(2,1)S(1)} collective-permute-done((bf16[128,1024]{1,0:T(8,128)(2,1)}, bf16[128,1024]{1,0:T(8,128)(2,1)S(1)}, u32[]{:S(2)}, u32[]{:S(2)}) %collective-permute-start.7) | collective-permute-done | bytes 262176 | tf_op jit(solution)/shard_map/ppermute | solution.py:79
  92.6 1.0 fusion.1._
  93.6 0.7 collective-permute-start.10
  94.3 0.7 collective-permute-start.9
  95.0 0.7 collective-permute-start.8
  95.7 1.3 fusion
  97.0 2.9 %collective-permute-start.12 = (bf16[512,256]{1,0:T(8,128)(2,1)S(1)}, bf16[512,256]{1,0:T(8,128)(2,1)S(1)}, u32[]{:S(2)}, u32[]{:S(2)}) collective-permute-start(bf16[512,256]{1,0:T(8,128)(2,1)S(1)} %fusion), channel_id=1, source_target_pairs={{0,128},{8,136},{16,144},{24,152},{32,160},{40,168},{48,176},{56,1... | collective-permute-start | bytes 786440 | tf_op jit(solution)/shard_map/ppermute | solution.py:79
  99.9 23.7 %shard_map.88 = (bf16[512,1024]{1,0:T(8,128)(2,1)}, bf16[512,1024]{1,0:T(8,128)(2,1)}, bf16[32,128,256]{2,1,0:T(8,128)(2,1)}, f32[768,256]{1,0:T(8,128)}, bf16[128,256]{1,0:T(8,128)(2,1)}) custom-call(s32[16]{0:T(128)} %pad_add_fusion.info, bf16[512,1024]{1,0:T(8,128)(2,1)} %q_ref.3, bf16[512,1024]{1,0:T(8,128)(2,1)} %g_ref.3, ...), custom_call_target="tpu_custom_call" | custom-call | flops 6442450944 | bytes 16777216 | tf_op jit(solution)/shard_map/pallas_call | solution.py:413
  123.7 0.7 copy-done.6
  124.4 0.7 copy-done.4
  125.1 11.1 %all-to-all-start.1 = ((bf16[32,128,256]{2,1,0:T(8,128)(2,1)}), bf16[32,128,256]{2,1,0:T(8,128)(2,1)S(1)}, u32[]{:S(2)}, u32[]{:S(2)}) async-start(bf16[32,128,256]{2,1,0:T(8,128)(2,1)} %get-tuple-element.45), calls=%async_computation.1 | async-start | bytes 4194304 | tf_op jit(solution)/shard_map/all_to_all | solution.py:599
  136.3 2.1 %collective-permute-start.14 = (bf16[128,256]{1,0:T(8,128)(2,1)S(1)}, bf16[128,256]{1,0:T(8,128)(2,1)S(1)}, u32[]{:S(2)}, u32[]{:S(2)}) collective-permute-start(bf16[128,256]{1,0:T(8,128)(2,1)S(1)} %copy-done.9), channel_id=1, source_target_pairs={{8,0},{240,248},{9,1},{241,249},{10,2},{242,250},{11,3},{243,251},... | collective-permute-start | bytes 196616 | tf_op jit(solution)/shard_map/ppermute | solution.py:79
  138.4 1.2 add_convert_fusion
  139.6 0.7 collective-permute-start.13
  140.3 0.9 broadcast_and_fusion
  141.2 0.9 slice_convert_fusion
  142.0 0.2 select_reduce_fusion.1
  142.2 0.1 select_reduce_fusion
  142.3 0.7 pad_add_fusion.1.target
  143.0 0.8 broadcast_select_fusion
  143.9 1.1 shard_map.89
  145.0 42.2 %all-to-all-done.1.recv_ref = bf16[32,128,256]{2,1,0:T(8,128)(2,1)S(1)} async-done(((bf16[32,128,256]{2,1,0:T(8,128)(2,1)}), bf16[32,128,256]{2,1,0:T(8,128)(2,1)S(1)}, u32[]{:S(2)}, u32[]{:S(2)}) %all-to-all-start.1) | async-done | bytes 2097184 | tf_op jit(solution)/shard_map/all_to_all | solution.py:599
  187.1 1.3 copy-done
  188.5 4.1 %shard_map.90 = (bf16[512,128]{1,0:T(8,128)(2,1)}, bf16[512,128]{1,0:T(8,128)(2,1)}) custom-call(s32[33]{0:T(128)} %pad_add_fusion.1.target, bf16[128,256]{1,0:T(8,128)(2,1)} %copy-done.7, f32[768,256]{1,0:T(8,128)} %get-tuple-element.42.own_ref, f32[512,256]{1,0:T(8,128)} %get-tuple-element.43.edge_ref, bf16[2,512,256]{2,1,0:T(8,128)(2,1)} %copy-done.2, ...), custom_call_target="tpu_custom_call" | custom-call | flops 1048576 | bytes 4194304 | tf_op jit(solution)/shard_map/pallas_call | solution.py:500
  (35 shorter events, 0.2 us)
Async XLA Ops:
  7.2 92.8 %all-gather.2.cloned.1.call-start = ((), (), s32[]{:S(2)}) async-start(), calls=%async_computation.2 | async-start | bytes 9191424 | tf_op jit(solution)/shard_map/all_gather | solution.py:552
  9.7 5.3 %copy-start.1 = (bf16[528,256]{1,0:T(8,128)(2,1)S(1)}, bf16[528,256]{1,0:T(8,128)(2,1)}, u32[]{:S(2)}) copy-start(bf16[528,256]{1,0:T(8,128)(2,1)} %shard_map.84._) | copy-start | bytes 811012
  12.9 5.7 %collective-permute-start.2 = (bf16[128,1024]{1,0:T(8,128)(2,1)}, bf16[128,1024]{1,0:T(8,128)(2,1)S(1)}, u32[]{:S(2)}, u32[]{:S(2)}) collective-permute-start(bf16[128,1024]{1,0:T(8,128)(2,1)} %get-tuple-element.26), channel_id=1, source_target_pairs={{0,64},{248,184},{1,65},{249,185},{2,66},{250,186},{3,67},{251,187... | collective-permute-start | bytes 786440 | tf_op jit(solution)/shard_map/ppermute | solution.py:79
  13.6 5.0 %collective-permute-start.3 = (bf16[128,1024]{1,0:T(8,128)(2,1)}, bf16[128,1024]{1,0:T(8,128)(2,1)S(1)}, u32[]{:S(2)}, u32[]{:S(2)}) collective-permute-start(bf16[128,1024]{1,0:T(8,128)(2,1)} %get-tuple-element.27), channel_id=1, source_target_pairs={{0,192},{248,56},{1,193},{249,57},{2,194},{250,58},{3,195},{251,59... | collective-permute-start | bytes 786440 | tf_op jit(solution)/shard_map/ppermute | solution.py:79
  14.3 4.4 %collective-permute-start.1 = (bf16[128,1024]{1,0:T(8,128)(2,1)}, bf16[128,1024]{1,0:T(8,128)(2,1)S(1)}, u32[]{:S(2)}, u32[]{:S(2)}) collective-permute-start(bf16[128,1024]{1,0:T(8,128)(2,1)} %get-tuple-element.27), channel_id=1, source_target_pairs={{0,128},{248,120},{1,129},{249,121},{2,130},{250,122},{3,131},{251... | collective-permute-start | bytes 786440 | tf_op jit(solution)/shard_map/ppermute | solution.py:79
  15.0 7.5 %collective-permute-start = (bf16[528,256]{1,0:T(8,128)(2,1)S(1)}, bf16[528,256]{1,0:T(8,128)(2,1)S(1)}, u32[]{:S(2)}, u32[]{:S(2)}) collective-permute-start(bf16[528,256]{1,0:T(8,128)(2,1)S(1)} %copy-done.1), channel_id=1, source_target_pairs={{0,128},{8,136},{16,144},{24,152},{32,160},{40,168},{48,176},{56,1... | collective-permute-start | bytes 811016 | tf_op jit(solution)/shard_map/ppermute | solution.py:79
  23.3 23.5 %collective-permute-start.6 = (bf16[1056,256]{1,0:T(8,128)(2,1)}, bf16[1056,256]{1,0:T(8,128)(2,1)S(1)}, u32[]{:S(2)}, u32[]{:S(2)}) collective-permute-start(bf16[1056,256]{1,0:T(8,128)(2,1)} %pad_maximum_fusion.both_ref), channel_id=1, source_target_pairs={{0,8},{8,0},{16,24},{24,16},{32,40},{40,32},{48,56},{56,48},{64,72... | collective-permute-start | bytes 1622024 | tf_op jit(solution)/shard_map/ppermute | solution.py:79
  37.0 0.7 collective-permute-start.4
  37.8 8.3 %collective-permute-start.5 = (bf16[128,1024]{1,0:T(8,128)(2,1)S(1)}, bf16[128,1024]{1,0:T(8,128)(2,1)S(1)}, u32[]{:S(2)}, u32[]{:S(2)}) collective-permute-start(bf16[128,1024]{1,0:T(8,128)(2,1)S(1)} %add.56), channel_id=1, source_target_pairs={{0,16},{32,48},{64,80},{96,112},{120,104},{88,72},{56,40},{24,8},{... | collective-permute-start | bytes 786440 | tf_op jit(solution)/shard_map/ppermute | solution.py:79
  46.8 0.8 copy-start.8
  71.4 24.3 %collective-permute-start.11 = (bf16[2,512,256]{2,1,0:T(8,128)(2,1)}, bf16[2,512,256]{2,1,0:T(8,128)(2,1)S(1)}, u32[]{:S(2)}, u32[]{:S(2)}) collective-permute-start(bf16[2,512,256]{2,1,0:T(8,128)(2,1)} %get-tuple-element.32), channel_id=1, source_target_pairs={{0,8},{8,0},{16,24},{24,16},{32,40},{40,32},{48,56},{56,48},{64,72... | collective-permute-start | bytes 1572872 | tf_op jit(solution)/shard_map/ppermute | solution.py:79
  81.2 11.4 %collective-permute-start.7 = (bf16[128,1024]{1,0:T(8,128)(2,1)}, bf16[128,1024]{1,0:T(8,128)(2,1)S(1)}, u32[]{:S(2)}, u32[]{:S(2)}) collective-permute-start(bf16[128,1024]{1,0:T(8,128)(2,1)} %get-tuple-element.30), channel_id=1, source_target_pairs={{16,0},{48,32},{80,64},{112,96},{104,120},{72,88},{40,56},{8,24},{... | collective-permute-start | bytes 786440 | tf_op jit(solution)/shard_map/ppermute | solution.py:79
  93.6 6.3 %copy-start.5 = (bf16[128,1024]{1,0:T(8,128)(2,1)}, bf16[128,1024]{1,0:T(8,128)(2,1)S(1)}, u32[]{:S(2)}) copy-start(bf16[128,1024]{1,0:T(8,128)(2,1)S(1)} %fusion.1._) | copy-start | bytes 786436
  93.6 30.0 %collective-permute-start.10 = (bf16[128,1024]{1,0:T(8,128)(2,1)S(1)}, bf16[128,1024]{1,0:T(8,128)(2,1)S(1)}, u32[]{:S(2)}, u32[]{:S(2)}) collective-permute-start(bf16[128,1024]{1,0:T(8,128)(2,1)S(1)} %fusion.1._), channel_id=1, source_target_pairs={{32,0},{88,120},{160,128},{216,248},{33,1},{89,121},{161,129},{217... | collective-permute-start | bytes 786440 | tf_op jit(solution)/shard_map/ppermute | solution.py:79
  94.3 29.4 %collective-permute-start.9 = (bf16[128,1024]{1,0:T(8,128)(2,1)S(1)}, bf16[128,1024]{1,0:T(8,128)(2,1)S(1)}, u32[]{:S(2)}, u32[]{:S(2)}) collective-permute-start(bf16[128,1024]{1,0:T(8,128)(2,1)S(1)} %fusion.1._), channel_id=1, source_target_pairs={{96,0},{24,120},{224,128},{152,248},{97,1},{25,121},{225,129},{153... | collective-permute-start | bytes 786440 | tf_op jit(solution)/shard_map/ppermute | solution.py:79
  95.0 28.7 %collective-permute-start.8 = (bf16[128,1024]{1,0:T(8,128)(2,1)S(1)}, bf16[128,1024]{1,0:T(8,128)(2,1)S(1)}, u32[]{:S(2)}, u32[]{:S(2)}) collective-permute-start(bf16[128,1024]{1,0:T(8,128)(2,1)S(1)} %fusion.1._), channel_id=1, source_target_pairs={{64,0},{56,120},{192,128},{184,248},{65,1},{57,121},{193,129},{185... | collective-permute-start | bytes 786440 | tf_op jit(solution)/shard_map/ppermute | solution.py:79
  95.7 28.0 %copy-start.2 = (bf16[2,512,256]{2,1,0:T(8,128)(2,1)}, bf16[2,512,256]{2,1,0:T(8,128)(2,1)S(1)}, u32[]{:S(2)}) copy-start(bf16[2,512,256]{2,1,0:T(8,128)(2,1)S(1)} %collective-permute-done.11.edge_core_ref) | copy-start | bytes 1572868
  97.0 26.7 %collective-permute-start.12 = (bf16[512,256]{1,0:T(8,128)(2,1)S(1)}, bf16[512,256]{1,0:T(8,128)(2,1)S(1)}, u32[]{:S(2)}, u32[]{:S(2)}) collective-permute-start(bf16[512,256]{1,0:T(8,128)(2,1)S(1)} %fusion), channel_id=1, source_target_pairs={{0,128},{8,136},{16,144},{24,152},{32,160},{40,168},{48,176},{56,1... | collective-permute-start | bytes 786440 | tf_op jit(solution)/shard_map/ppermute | solution.py:79
  123.7 0.7 copy-start.6
  124.4 0.7 copy-start.4
  124.4 11.9 %copy-start.9 = (bf16[128,256]{1,0:T(8,128)(2,1)S(1)}, bf16[128,256]{1,0:T(8,128)(2,1)}, u32[]{:S(2)}) copy-start(bf16[128,256]{1,0:T(8,128)(2,1)} %get-tuple-element.41) | copy-start | bytes 196612
  124.4 14.0 %copy-start.3 = (bf16[128,1024]{1,0:T(8,128)(2,1)S(1)}, bf16[128,1024]{1,0:T(8,128)(2,1)}, u32[]{:S(2)}) copy-start(bf16[128,1024]{1,0:T(8,128)(2,1)} %get-tuple-element.30) | copy-start | bytes 786436
  125.1 62.0 %all-to-all-start.1 = ((bf16[32,128,256]{2,1,0:T(8,128)(2,1)}), bf16[32,128,256]{2,1,0:T(8,128)(2,1)S(1)}, u32[]{:S(2)}, u32[]{:S(2)}) async-start(bf16[32,128,256]{2,1,0:T(8,128)(2,1)} %get-tuple-element.45), calls=%async_computation.1 | async-start | bytes 4194304 | tf_op jit(solution)/shard_map/all_to_all | solution.py:599
  136.3 8.7 %collective-permute-start.14 = (bf16[128,256]{1,0:T(8,128)(2,1)S(1)}, bf16[128,256]{1,0:T(8,128)(2,1)S(1)}, u32[]{:S(2)}, u32[]{:S(2)}) collective-permute-start(bf16[128,256]{1,0:T(8,128)(2,1)S(1)} %copy-done.9), channel_id=1, source_target_pairs={{8,0},{240,248},{9,1},{241,249},{10,2},{242,250},{11,3},{243,251},... | collective-permute-start | bytes 196616 | tf_op jit(solution)/shard_map/ppermute | solution.py:79
  139.6 3.4 %collective-permute-start.13 = (bf16[128,1024]{1,0:T(8,128)(2,1)S(1)}, bf16[128,1024]{1,0:T(8,128)(2,1)S(1)}, u32[]{:S(2)}, u32[]{:S(2)}) collective-permute-start(bf16[128,1024]{1,0:T(8,128)(2,1)S(1)} %add_convert_fusion), channel_id=1, source_target_pairs={{128,0},{120,248},{129,1},{121,249},{130,2},{122,250},{131,3},{123... | collective-permute-start | bytes 786440 | tf_op jit(solution)/shard_map/ppermute | solution.py:79
  145.0 42.2 %copy-start.7 = (bf16[128,256]{1,0:T(8,128)(2,1)}, bf16[128,256]{1,0:T(8,128)(2,1)S(1)}, u32[]{:S(2)}) copy-start(bf16[128,256]{1,0:T(8,128)(2,1)S(1)} %collective-permute-done.14.extra_ref) | copy-start | bytes 196612
  187.1 1.3 copy-start
Sparse Core Ops, SparseCore 0:
  23.5 70.8 all-gather.1

commit v2 on v1

--- a/solution.py
+++ b/solution.py
@@ -22,7 +22,7 @@
 SCALE = 1.0 / math.sqrt(D)
 LOG2E = math.log2(math.e)
 FAR = -1e30
-VMEM_LIMIT = 56 * 1024 * 1024
+MIB = 1 << 20
 NT = (((1,), (1,)), ((), ()))
 TN = (((0,), (0,)), ((), ()))
 
@@ -431,7 +431,7 @@
             pltpu.SemaphoreType.DMA((2, SLOTS)),
             pltpu.SemaphoreType.DMA((QB + 1, 4)),
         ],
-        compiler_params=pltpu.CompilerParams(vmem_limit_bytes=VMEM_LIMIT),
+        compiler_params=pltpu.CompilerParams(vmem_limit_bytes=56 * MIB),
         cost_estimate=pl.CostEstimate(
             flops=QB * 6 * 2 * KEYS * HEADS * B * D,
             bytes_accessed=QB * (4 << 20),
@@ -440,37 +440,8 @@
     )(info, query_rows, out_grad, gathered, later)
 
 
-def sum_kernel(
-    target,
-    extra_ref,
-    own_ref,
-    edge_ref,
-    edge_core_ref,
-    edge_across_ref,
-    recv_ref,
-    dk_ref,
-    dv_ref,
-    acc,
-    held,
-    sems,
-):
-    def copy(s):
-        return pltpu.make_async_copy(recv_ref.at[s], held.at[s], sems.at[s])
-
-    def begin(s, carry):
-        @pl.when(target[s] >= 0)
-        def _():
-            copy(s).start()
-
-        return carry
-
-    lax.fori_loop(0, SEQ, begin, 0)
-    acc[...] = (
-        own_ref[:ROWS, :]
-        + edge_ref[...]
-        + edge_core_ref[0].astype(jnp.float32)
-        + edge_across_ref[...].astype(jnp.float32)
-    )
+def sum_kernel(target, extra_ref, base_ref, recv_ref, dk_ref, dv_ref, acc):
+    acc[...] = base_ref[...]
     t = target[SEQ]
 
     @pl.when(t >= 0)
@@ -483,9 +454,8 @@
 
         @pl.when(t >= 0)
         def _():
-            copy(s).wait()
             rows = pl.ds(pl.multiple_of(t * B, B), B)
-            acc[rows, :] += held[s].astype(jnp.float32)
+            acc[rows, :] += recv_ref[s].astype(jnp.float32)
 
         return carry
 
@@ -494,7 +464,9 @@
     dv_ref[...] = acc[:, D:].astype(jnp.bfloat16)
 
 
-def call(kernel, outs, args, scalars=0, later=0, scratch=(), flops=0, bytes_accessed=0, exps=0):
+def call(
+    kernel, outs, args, vmem_mib, scalars=0, later=0, scratch=(), flops=0, bytes_accessed=0, exps=0
+):
     vmem = pl.BlockSpec(memory_space=pltpu.VMEM)
     smem = pl.BlockSpec(memory_space=pltpu.SMEM)
     return pl.pallas_call(
@@ -505,7 +477,7 @@
         + [pl.BlockSpec(memory_space=pl.ANY)] * later,
         out_specs=[vmem] * len(outs),
         scratch_shapes=list(scratch),
-        compiler_params=pltpu.CompilerParams(vmem_limit_bytes=VMEM_LIMIT),
+        compiler_params=pltpu.CompilerParams(vmem_limit_bytes=vmem_mib * MIB),
         cost_estimate=pl.CostEstimate(
             flops=flops, bytes_accessed=bytes_accessed, transcendentals=exps
         ),
@@ -531,6 +503,7 @@
         pack_kernel,
         [((PIECE, 2 * D), bf16)],
         [random_blocks, key_rows, value_rows],
+        56,
         scalars=1,
         bytes_accessed=1 << 19,
     )
@@ -541,6 +514,7 @@
         in_specs=[smem, anywhere, anywhere, anywhere],
         out_specs=[vmem, vmem],
         scratch_shapes=[pltpu.SemaphoreType.DMA((2, 2))],
+        compiler_params=pltpu.CompilerParams(vmem_limit_bytes=56 * MIB),
         cost_estimate=pl.CostEstimate(flops=0, bytes_accessed=1 << 27, transcendentals=0),
     )(info, query_rows, out_grad, mine)
 
@@ -559,6 +533,7 @@
         edge_stats_kernel,
         [((8, 4 * D), f32)],
         [edge] + near,
+        24,
         flops=2 * edge_flops,
         bytes_accessed=2 << 20,
         exps=4 * ROWS * ROWS,
@@ -575,6 +550,7 @@
             ((ROWS, 2 * D), f32),
         ],
         [edge] + near + [all_stats],
+        24,
         flops=6 * edge_flops,
         bytes_accessed=4 << 20,
         exps=4 * ROWS * ROWS,
@@ -614,17 +590,14 @@
     extra_at = jnp.where(me == 0, QB - 1, jnp.where(me == SEQ - 1, 0, -1))
     target = jnp.concatenate([by_source, extra_at[None]]).astype(jnp.int32)
 
+    base = own[:ROWS] + edge_mine + edge_core[0].astype(f32) + edge_across.astype(f32)
     key_grad, value_grad = call(
         sum_kernel,
         [((ROWS, D), bf16), ((ROWS, D), bf16)],
-        [target, extra, own, edge_mine, edge_core, edge_across, recv],
+        [target, extra, base, recv],
+        12,
         scalars=1,
-        later=1,
-        scratch=[
-            pltpu.VMEM((ROWS, 2 * D), f32),
-            pltpu.VMEM((SEQ, B, 2 * D), bf16),
-            pltpu.SemaphoreType.DMA((SEQ,)),
-        ],
+        scratch=[pltpu.VMEM((ROWS, 2 * D), f32)],
         flops=1 << 20,
         bytes_accessed=4 << 20,
     )
@@ -640,6 +613,7 @@
         out_specs=[anywhere, anywhere],
         input_output_aliases={3: 0, 4: 1},
         scratch_shapes=[pltpu.SemaphoreType.DMA((2, 2))],
+        compiler_params=pltpu.CompilerParams(vmem_limit_bytes=8 * MIB),
         cost_estimate=pl.CostEstimate(flops=0, bytes_accessed=1 << 20, transcendentals=0),
     )(info, low, high, attended, query_grad)
     return attended, query_grad, key_grad, value_grad

time: 201 us -> 193 us (0.960)
  Pallas kernels: 42.2 us -> 35.2 us
  local copies, waits for them, and re-layouts: 5.05 us -> 1.67 us
  waiting for transfers between devices: 62.2 us -> 65 us
  other arithmetic: 9.37 us -> 7.33 us
    pallas_call x4, Pallas kernels: 14.8 us -> 8.21 us  [call(): pl.pallas_call(kernel, out_shape=[jax.ShapeDtypeStruct(shape, dtype) for...]
    unnamed x20 -> x18, local copies, waits for them, and re-layouts: 3.56 us -> 0.9 us
    all_gather x1, waiting for transfers between devices: 0.01 us -> 2.52 us  [local(): lax.all_gather(both, 'seq', axis_index_groups=ZC_GROUPS, tiled=True)]
  transfers between devices with their start and end apart: 17 -> 17, of which waited for: 4 -> 5; matrix products, arithmetic and copies ran while one was open for 4% -> 3% of each run, Pallas kernels for 17% -> 15%
where the time goes in v2:
time: 193 us; the launch traced here: 190 us
  waiting for transfers between devices  65 us (34%)
  starting transfers between devices  52.6 us (27%)
  Pallas kernels  35.2 us (18%)
  between operations  14.4 us (7%)
  blocking collectives  13.8 us (7%)
  other arithmetic  7.33 us (4%)
    all_to_all x1, waiting for transfers between devices, local(): recv = lax.all_to_all(send, 'seq', 0, 0)  42.7 us
    ppermute x15, starting transfers between devices, permute(): return lax.ppermute(value, 'seq', pairs)  42.2 us
    pallas_call x1, Pallas kernels, middle_call(): pl.pallas_call(middle_kernel, grid=(QB,), out_shape=[jax.ShapeDtypeStruct...  23.8 us
    ppermute x15, waiting for transfers between devices, permute(): return lax.ppermute(value, 'seq', pairs)  19.8 us
    all_to_all x1, blocking collectives, local(): lax.all_to_all(jnp.broadcast_to(stats, (ZN, *stats.shape)), 'seq', 0, 0,...  13.8 us
    all_to_all x1, starting transfers between devices, local(): recv = lax.all_to_all(send, 'seq', 0, 0)  10.4 us
    pallas_call x4, Pallas kernels, call(): pl.pallas_call(kernel, out_shape=[jax.ShapeDtypeStruct(shape, dtype) for...  8.21 us
  transfers between devices with their start and end apart: 17, of which 5 were waited for; matrix products, arithmetic and copies ran while one was open for 3% of the time, Pallas kernels for 15%

profile of v2, /device:TPU:1, one launch (start us, length us, event | category | flops | bytes accessed | tf_op | source)
XLA Modules:
  0.0 190.1 jit_solution(8738889211131309306)
XLA Ops:
  7.2 0.0 all-gather.2.cloned.1.call-start
  7.2 0.8 reshape.80
  8.0 1.7 shard_map.84._
  9.7 0.7 pad_add_fusion.info
  10.4 2.6 %shard_map.85 = (bf16[128,1024]{1,0:T(8,128)(2,1)}, bf16[128,1024]{1,0:T(8,128)(2,1)}) custom-call(s32[16]{0:T(128)} %pad_add_fusion.info, bf16[512,1024]{1,0:T(8,128)(2,1)} %q_ref.3, bf16[512,1024]{1,0:T(8,128)(2,1)} %g_ref.3, bf16[528,256]{1,0:T(8,128)(2,1)} %shard_map.84._), custom_call_target="tpu_custom_call" | custom-call | bytes 134217728 | tf_op jit(solution)/shard_map/pallas_call | solution.py:511
  13.0 0.7 collective-permute-start.2
  13.7 0.7 collective-permute-start.3
  14.4 0.7 collective-permute-start.1
  15.1 3.7 %collective-permute-start = (bf16[528,256]{1,0:T(8,128)(2,1)S(1)}, bf16[528,256]{1,0:T(8,128)(2,1)S(1)}, u32[]{:S(2)}, u32[]{:S(2)}) collective-permute-start(bf16[528,256]{1,0:T(8,128)(2,1)S(1)} %copy-done.2), channel_id=1, source_target_pairs={{0,128},{8,136},{16,144},{24,152},{32,160},{40,168},{48,176},{56,1... | collective-permute-start | bytes 811016 | tf_op jit(solution)/shard_map/ppermute | solution.py:79
  18.7 0.1 add_add_fusion
  18.8 3.8 %collective-permute-done = bf16[528,256]{1,0:T(8,128)(2,1)S(1)} collective-permute-done((bf16[528,256]{1,0:T(8,128)(2,1)S(1)}, bf16[528,256]{1,0:T(8,128)(2,1)S(1)}, u32[]{:S(2)}, u32[]{:S(2)}) %collective-permute-start) | collective-permute-done | bytes 270368 | tf_op jit(solution)/shard_map/ppermute | solution.py:79
  22.6 0.8 pad_maximum_fusion.both_ref
  23.4 13.7 %collective-permute-start.6 = (bf16[1056,256]{1,0:T(8,128)(2,1)}, bf16[1056,256]{1,0:T(8,128)(2,1)S(1)}, u32[]{:S(2)}, u32[]{:S(2)}) collective-permute-start(bf16[1056,256]{1,0:T(8,128)(2,1)} %pad_maximum_fusion.both_ref), channel_id=1, source_target_pairs={{0,8},{8,0},{16,24},{24,16},{32,40},{40,32},{48,56},{56,48},{64,72... | collective-permute-start | bytes 1622024 | tf_op jit(solution)/shard_map/ppermute | solution.py:79
  37.1 0.7 collective-permute-start.4
  37.8 0.1 add.65
  37.8 1.3 collective-permute-start.5
  39.1 7.1 %collective-permute-done.5 = bf16[128,1024]{1,0:T(8,128)(2,1)S(1)} collective-permute-done((bf16[128,1024]{1,0:T(8,128)(2,1)S(1)}, bf16[128,1024]{1,0:T(8,128)(2,1)S(1)}, u32[]{:S(2)}, u32[]{:S(2)}) %collective-permute-start.5) | collective-permute-done | bytes 262176 | tf_op jit(solution)/shard_map/ppermute | solution.py:79
  46.3 0.1 add.66.edge_ref
  46.4 1.6 shard_map.86
  48.0 13.8 %all_to_all.10.stats_ref = f32[8,8,512]{2,1,0:T(8,128)S(1)} all-to-all(f32[8,8,512]{2,1,0:T(8,128)S(1)} %broadcast_in_dim.48), channel_id=1, replica_groups={{0,16,32,48,64,80,96,112},{8,24,40,56,72,88,104,120},{128,144,160,176,1..., dimensions={0} | all-to-all | bytes 262144 | tf_op jit(solution)/shard_map/all_to_all | solution.py:541
  61.8 3.0 %shard_map.87 = (bf16[128,1024]{1,0:T(8,128)(2,1)S(1)}, f32[512,256]{1,0:T(8,128)S(1)}, bf16[2,512,256]{2,1,0:T(8,128)(2,1)S(1)}, f32[512,256]{1,0:T(8,128)S(1)}) custom-call(bf16[128,1024]{1,0:T(8,128)(2,1)S(1)} %add.66.edge_ref, bf16[1056,256]{1,0:T(8,128)(2,1)S(1)} %copy-done, bf16[1056,256]{1,0:T(8,128)(2,1)S(1)} %collective-permute-done.6.other_ref, ...), custom_call_target="tpu_custom_call" | custom-call | flops 1610612736 | bytes 4194304 | tf_op jit(solution)/shard_map/pallas_call | solution.py:472
  64.8 10.2 %collective-permute-start.11 = (bf16[2,512,256]{2,1,0:T(8,128)(2,1)S(1)}, bf16[2,512,256]{2,1,0:T(8,128)(2,1)S(1)}, u32[]{:S(2)}, u32[]{:S(2)}) collective-permute-start(bf16[2,512,256]{2,1,0:T(8,128)(2,1)S(1)} %get-tuple-element.32), channel_id=1, source_target_pairs={{0,8},{8,0},{16,24},{24,16},{32,40},{40,32},{48,56},{56,48},{64,72... | collective-permute-start | bytes 1572872 | tf_op jit(solution)/shard_map/ppermute | solution.py:79
  75.0 2.2 %collective-permute-start.7 = (bf16[128,1024]{1,0:T(8,128)(2,1)S(1)}, bf16[128,1024]{1,0:T(8,128)(2,1)S(1)}, u32[]{:S(2)}, u32[]{:S(2)}) collective-permute-start(bf16[128,1024]{1,0:T(8,128)(2,1)S(1)} %get-tuple-element.30), channel_id=1, source_target_pairs={{16,0},{48,32},{80,64},{112,96},{104,120},{72,88},{40,56},{8,24},{... | collective-permute-start | bytes 786440 | tf_op jit(solution)/shard_map/ppermute | solution.py:79
  77.2 8.9 %collective-permute-done.7 = bf16[128,1024]{1,0:T(8,128)(2,1)S(1)} collective-permute-done((bf16[128,1024]{1,0:T(8,128)(2,1)S(1)}, bf16[128,1024]{1,0:T(8,128)(2,1)S(1)}, u32[]{:S(2)}, u32[]{:S(2)}) %collective-permute-start.7) | collective-permute-done | bytes 262176 | tf_op jit(solution)/shard_map/ppermute | solution.py:79
  86.1 0.1 fusion.2._
  86.2 0.7 collective-permute-start.10
  86.9 0.7 collective-permute-start.9
  87.6 0.7 collective-permute-start.8
  88.3 0.8 fusion.1
  89.1 3.6 %collective-permute-start.12 = (bf16[512,256]{1,0:T(8,128)(2,1)}, bf16[512,256]{1,0:T(8,128)(2,1)S(1)}, u32[]{:S(2)}, u32[]{:S(2)}) collective-permute-start(bf16[512,256]{1,0:T(8,128)(2,1)} %fusion.1), channel_id=1, source_target_pairs={{0,128},{8,136},{16,144},{24,152},{32,160},{40,168},{48,176},{56,1... | collective-permute-start | bytes 786440 | tf_op jit(solution)/shard_map/ppermute | solution.py:79
  92.7 2.5 %all-gather.2.cloned.1.call-done.all_ref = bf16[16896,256]{1,0:T(8,128)(2,1)} async-done(((bf16[1056,256]{1,0:T(8,128)(2,1)}), bf16[16896,256]{1,0:T(8,128)(2,1)}) %all-gather.2.cloned.1.call-update) | async-done | bytes 8650768 | tf_op jit(solution)/shard_map/all_gather | solution.py:526
  95.2 23.8 %shard_map.88 = (bf16[512,1024]{1,0:T(8,128)(2,1)}, bf16[512,1024]{1,0:T(8,128)(2,1)}, bf16[32,128,256]{2,1,0:T(8,128)(2,1)}, f32[768,256]{1,0:T(8,128)}, bf16[128,256]{1,0:T(8,128)(2,1)}) custom-call(s32[16]{0:T(128)} %pad_add_fusion.info, bf16[512,1024]{1,0:T(8,128)(2,1)} %q_ref.3, bf16[512,1024]{1,0:T(8,128)(2,1)} %g_ref.3, ...), custom_call_target="tpu_custom_call" | custom-call | flops 6442450944 | bytes 16777216 | tf_op jit(solution)/shard_map/pallas_call | solution.py:413
  119.2 0.7 copy-done.5
  119.8 0.1 copy-done.6
  119.9 0.1 copy-done.7
  120.0 10.4 %all-to-all-start.1 = ((bf16[32,128,256]{2,1,0:T(8,128)(2,1)}), bf16[32,128,256]{2,1,0:T(8,128)(2,1)S(1)}, u32[]{:S(2)}, u32[]{:S(2)}) async-start(bf16[32,128,256]{2,1,0:T(8,128)(2,1)} %get-tuple-element.45), calls=%async_computation.1 | async-start | bytes 4194304 | tf_op jit(solution)/shard_map/all_to_all | solution.py:575
  130.5 2.1 %collective-permute-start.14 = (bf16[128,256]{1,0:T(8,128)(2,1)S(1)}, bf16[128,256]{1,0:T(8,128)(2,1)S(1)}, u32[]{:S(2)}, u32[]{:S(2)}) collective-permute-start(bf16[128,256]{1,0:T(8,128)(2,1)S(1)} %copy-done.8), channel_id=1, source_target_pairs={{8,0},{240,248},{9,1},{241,249},{10,2},{242,250},{11,3},{243,251},... | collective-permute-start | bytes 196616 | tf_op jit(solution)/shard_map/ppermute | solution.py:79
  132.6 1.2 add_convert_fusion
  133.9 0.7 collective-permute-start.13
  134.6 0.9 broadcast_and_fusion
  135.4 0.9 slice_convert_fusion
  136.3 0.2 select_reduce_fusion.1
  136.5 0.1 select_reduce_fusion
  136.6 0.1 pad_add_fusion.1.target
  136.7 1.3 fusion.base_ref
  138.0 0.6 shard_map.89
  138.7 42.7 %all-to-all-done.1.recv_ref = bf16[32,128,256]{2,1,0:T(8,128)(2,1)S(1)} async-done(((bf16[32,128,256]{2,1,0:T(8,128)(2,1)}), bf16[32,128,256]{2,1,0:T(8,128)(2,1)S(1)}, u32[]{:S(2)}, u32[]{:S(2)}) %all-to-all-start.1) | async-done | bytes 2097184 | tf_op jit(solution)/shard_map/all_to_all | solution.py:575
  181.3 1.9 shard_map.90
  (34 shorter events, 0.2 us)
Async XLA Ops:
  7.2 88.1 %all-gather.2.cloned.1.call-start = ((), (), s32[]{:S(2)}) async-start(), calls=%async_computation.2 | async-start | bytes 9191424 | tf_op jit(solution)/shard_map/all_gather | solution.py:526
  9.7 5.3 %copy-start.2 = (bf16[528,256]{1,0:T(8,128)(2,1)S(1)}, bf16[528,256]{1,0:T(8,128)(2,1)}, u32[]{:S(2)}) copy-start(bf16[528,256]{1,0:T(8,128)(2,1)} %shard_map.84._) | copy-start | bytes 811012
  13.0 5.7 %collective-permute-start.2 = (bf16[128,1024]{1,0:T(8,128)(2,1)}, bf16[128,1024]{1,0:T(8,128)(2,1)S(1)}, u32[]{:S(2)}, u32[]{:S(2)}) collective-permute-start(bf16[128,1024]{1,0:T(8,128)(2,1)} %get-tuple-element.26), channel_id=1, source_target_pairs={{0,64},{248,184},{1,65},{249,185},{2,66},{250,186},{3,67},{251,187... | collective-permute-start | bytes 786440 | tf_op jit(solution)/shard_map/ppermute | solution.py:79
  13.7 5.0 %collective-permute-start.3 = (bf16[128,1024]{1,0:T(8,128)(2,1)}, bf16[128,1024]{1,0:T(8,128)(2,1)S(1)}, u32[]{:S(2)}, u32[]{:S(2)}) collective-permute-start(bf16[128,1024]{1,0:T(8,128)(2,1)} %get-tuple-element.27), channel_id=1, source_target_pairs={{0,192},{248,56},{1,193},{249,57},{2,194},{250,58},{3,195},{251,59... | collective-permute-start | bytes 786440 | tf_op jit(solution)/shard_map/ppermute | solution.py:79
  14.4 4.4 %collective-permute-start.1 = (bf16[128,1024]{1,0:T(8,128)(2,1)}, bf16[128,1024]{1,0:T(8,128)(2,1)S(1)}, u32[]{:S(2)}, u32[]{:S(2)}) collective-permute-start(bf16[128,1024]{1,0:T(8,128)(2,1)} %get-tuple-element.27), channel_id=1, source_target_pairs={{0,128},{248,120},{1,129},{249,121},{2,130},{250,122},{3,131},{251... | collective-permute-start | bytes 786440 | tf_op jit(solution)/shard_map/ppermute | solution.py:79
  15.1 7.5 %collective-permute-start = (bf16[528,256]{1,0:T(8,128)(2,1)S(1)}, bf16[528,256]{1,0:T(8,128)(2,1)S(1)}, u32[]{:S(2)}, u32[]{:S(2)}) collective-permute-start(bf16[528,256]{1,0:T(8,128)(2,1)S(1)} %copy-done.2), channel_id=1, source_target_pairs={{0,128},{8,136},{16,144},{24,152},{32,160},{40,168},{48,176},{56,1... | collective-permute-start | bytes 811016 | tf_op jit(solution)/shard_map/ppermute | solution.py:79
  23.4 23.0 %copy-start = (bf16[1056,256]{1,0:T(8,128)(2,1)S(1)}, bf16[1056,256]{1,0:T(8,128)(2,1)}, u32[]{:S(2)}) copy-start(bf16[1056,256]{1,0:T(8,128)(2,1)} %pad_maximum_fusion.both_ref) | copy-start | bytes 1622020
  23.4 22.9 %collective-permute-start.6 = (bf16[1056,256]{1,0:T(8,128)(2,1)}, bf16[1056,256]{1,0:T(8,128)(2,1)S(1)}, u32[]{:S(2)}, u32[]{:S(2)}) collective-permute-start(bf16[1056,256]{1,0:T(8,128)(2,1)} %pad_maximum_fusion.both_ref), channel_id=1, source_target_pairs={{0,8},{8,0},{16,24},{24,16},{32,40},{40,32},{48,56},{56,48},{64,72... | collective-permute-start | bytes 1622024 | tf_op jit(solution)/shard_map/ppermute | solution.py:79
  37.1 0.7 collective-permute-start.4
  37.8 8.4 %collective-permute-start.5 = (bf16[128,1024]{1,0:T(8,128)(2,1)S(1)}, bf16[128,1024]{1,0:T(8,128)(2,1)S(1)}, u32[]{:S(2)}, u32[]{:S(2)}) collective-permute-start(bf16[128,1024]{1,0:T(8,128)(2,1)S(1)} %add.65), channel_id=1, source_target_pairs={{0,16},{32,48},{64,80},{96,112},{120,104},{88,72},{56,40},{24,8},{... | collective-permute-start | bytes 786440 | tf_op jit(solution)/shard_map/ppermute | solution.py:79
  64.8 23.5 %collective-permute-start.11 = (bf16[2,512,256]{2,1,0:T(8,128)(2,1)S(1)}, bf16[2,512,256]{2,1,0:T(8,128)(2,1)S(1)}, u32[]{:S(2)}, u32[]{:S(2)}) collective-permute-start(bf16[2,512,256]{2,1,0:T(8,128)(2,1)S(1)} %get-tuple-element.32), channel_id=1, source_target_pairs={{0,8},{8,0},{16,24},{24,16},{32,40},{40,32},{48,56},{56,48},{64,72... | collective-permute-start | bytes 1572872 | tf_op jit(solution)/shard_map/ppermute | solution.py:79
  75.0 11.1 %collective-permute-start.7 = (bf16[128,1024]{1,0:T(8,128)(2,1)S(1)}, bf16[128,1024]{1,0:T(8,128)(2,1)S(1)}, u32[]{:S(2)}, u32[]{:S(2)}) collective-permute-start(bf16[128,1024]{1,0:T(8,128)(2,1)S(1)} %get-tuple-element.30), channel_id=1, source_target_pairs={{16,0},{48,32},{80,64},{112,96},{104,120},{72,88},{40,56},{8,24},{... | collective-permute-start | bytes 786440 | tf_op jit(solution)/shard_map/ppermute | solution.py:79
  86.2 9.1 %copy-start.4 = (bf16[128,1024]{1,0:T(8,128)(2,1)}, bf16[128,1024]{1,0:T(8,128)(2,1)S(1)}, u32[]{:S(2)}) copy-start(bf16[128,1024]{1,0:T(8,128)(2,1)S(1)} %fusion.2._) | copy-start | bytes 786436
  86.2 32.9 %collective-permute-start.10 = (bf16[128,1024]{1,0:T(8,128)(2,1)S(1)}, bf16[128,1024]{1,0:T(8,128)(2,1)S(1)}, u32[]{:S(2)}, u32[]{:S(2)}) collective-permute-start(bf16[128,1024]{1,0:T(8,128)(2,1)S(1)} %fusion.2._), channel_id=1, source_target_pairs={{32,0},{88,120},{160,128},{216,248},{33,1},{89,121},{161,129},{217... | collective-permute-start | bytes 786440 | tf_op jit(solution)/shard_map/ppermute | solution.py:79
  86.9 32.2 %collective-permute-start.9 = (bf16[128,1024]{1,0:T(8,128)(2,1)S(1)}, bf16[128,1024]{1,0:T(8,128)(2,1)S(1)}, u32[]{:S(2)}, u32[]{:S(2)}) collective-permute-start(bf16[128,1024]{1,0:T(8,128)(2,1)S(1)} %fusion.2._), channel_id=1, source_target_pairs={{96,0},{24,120},{224,128},{152,248},{97,1},{25,121},{225,129},{153... | collective-permute-start | bytes 786440 | tf_op jit(solution)/shard_map/ppermute | solution.py:79
  87.6 31.6 %collective-permute-start.8 = (bf16[128,1024]{1,0:T(8,128)(2,1)S(1)}, bf16[128,1024]{1,0:T(8,128)(2,1)S(1)}, u32[]{:S(2)}, u32[]{:S(2)}) collective-permute-start(bf16[128,1024]{1,0:T(8,128)(2,1)S(1)} %fusion.2._), channel_id=1, source_target_pairs={{64,0},{56,120},{192,128},{184,248},{65,1},{57,121},{193,129},{185... | collective-permute-start | bytes 786440 | tf_op jit(solution)/shard_map/ppermute | solution.py:79
  88.3 30.8 %copy-start.3 = (bf16[2,512,256]{2,1,0:T(8,128)(2,1)}, bf16[2,512,256]{2,1,0:T(8,128)(2,1)S(1)}, u32[]{:S(2)}) copy-start(bf16[2,512,256]{2,1,0:T(8,128)(2,1)S(1)} %collective-permute-done.11) | copy-start | bytes 1572868
  89.1 30.0 %collective-permute-start.12 = (bf16[512,256]{1,0:T(8,128)(2,1)}, bf16[512,256]{1,0:T(8,128)(2,1)S(1)}, u32[]{:S(2)}, u32[]{:S(2)}) collective-permute-start(bf16[512,256]{1,0:T(8,128)(2,1)} %fusion.1), channel_id=1, source_target_pairs={{0,128},{8,136},{16,144},{24,152},{32,160},{40,168},{48,176},{56,1... | collective-permute-start | bytes 786440 | tf_op jit(solution)/shard_map/ppermute | solution.py:79
  119.1 0.7 copy-start.5
  119.1 0.8 copy-start.6
  119.1 0.9 copy-start.7
  119.2 11.3 %copy-start.8 = (bf16[128,256]{1,0:T(8,128)(2,1)S(1)}, bf16[128,256]{1,0:T(8,128)(2,1)}, u32[]{:S(2)}) copy-start(bf16[128,256]{1,0:T(8,128)(2,1)} %get-tuple-element.41) | copy-start | bytes 196612
  120.0 61.3 %all-to-all-start.1 = ((bf16[32,128,256]{2,1,0:T(8,128)(2,1)}), bf16[32,128,256]{2,1,0:T(8,128)(2,1)S(1)}, u32[]{:S(2)}, u32[]{:S(2)}) async-start(bf16[32,128,256]{2,1,0:T(8,128)(2,1)} %get-tuple-element.45), calls=%async_computation.1 | async-start | bytes 4194304 | tf_op jit(solution)/shard_map/all_to_all | solution.py:575
  130.5 7.6 %copy-start.1 = (s32[16]{0:T(128)S(1)}, s32[16]{0:T(128)}, u32[]{:S(2)}) copy-start(s32[16]{0:T(128)} %pad_add_fusion.info) | copy-start | bytes 196
  130.5 8.2 %collective-permute-start.14 = (bf16[128,256]{1,0:T(8,128)(2,1)S(1)}, bf16[128,256]{1,0:T(8,128)(2,1)S(1)}, u32[]{:S(2)}, u32[]{:S(2)}) collective-permute-start(bf16[128,256]{1,0:T(8,128)(2,1)S(1)} %copy-done.8), channel_id=1, source_target_pairs={{8,0},{240,248},{9,1},{241,249},{10,2},{242,250},{11,3},{243,251},... | collective-permute-start | bytes 196616 | tf_op jit(solution)/shard_map/ppermute | solution.py:79
  133.9 4.1 %collective-permute-start.13 = (bf16[128,1024]{1,0:T(8,128)(2,1)S(1)}, bf16[128,1024]{1,0:T(8,128)(2,1)S(1)}, u32[]{:S(2)}, u32[]{:S(2)}) collective-permute-start(bf16[128,1024]{1,0:T(8,128)(2,1)S(1)} %add_convert_fusion), channel_id=1, source_target_pairs={{128,0},{120,248},{129,1},{121,249},{130,2},{122,250},{131,3},{123... | collective-permute-start | bytes 786440 | tf_op jit(solution)/shard_map/ppermute | solution.py:79
Sparse Core Ops, SparseCore 0:
  23.5 71.6 all-gather.1

commit v3 on v2

--- a/solution.py
+++ b/solution.py
@@ -89,19 +89,8 @@
     )
 
 
-def pack_kernel(ids_ref, k_ref, v_ref, mine_ref):
-    mine_ref[:ROWS, :D] = k_ref[...]
-    mine_ref[:ROWS, D:] = v_ref[...]
-    shape = (PIECE - ROWS, 2 * D)
-    column = lax.broadcasted_iota(jnp.int32, shape, 1)
-    ids = jnp.zeros(shape, jnp.int32)
-    for n in range(QB * 3):
-        ids = jnp.where(column == n, ids_ref[n // 3, n % 3], ids)
-    mine_ref[ROWS:, :] = ids.astype(jnp.float32).astype(jnp.bfloat16)
-
-
-def edge_kernel(info, q_ref, g_ref, _, own_ref, other_ref, sems):
-    me = info[12]
+def pack_kernel(ids_ref, k_ref, v_ref, q_ref, g_ref, mine_ref, own_ref, other_ref, sems):
+    me = lax.axis_index("seq")
     start = pl.multiple_of((me & 1) * (ROWS - B), B)
     copies = []
     for side, out in enumerate((own_ref, other_ref)):
@@ -116,6 +105,14 @@
             )
     for copy in copies:
         copy.start()
+    mine_ref[:ROWS, :D] = k_ref[...]
+    mine_ref[:ROWS, D:] = v_ref[...]
+    shape = (PIECE - ROWS, 2 * D)
+    column = lax.broadcasted_iota(jnp.int32, shape, 1)
+    ids = jnp.zeros(shape, jnp.int32)
+    for n in range(QB * 3):
+        ids = jnp.where(column == n, ids_ref[n // 3, n % 3], ids)
+    mine_ref[ROWS:, :] = ids.astype(jnp.float32).astype(jnp.bfloat16)
     for copy in copies:
         copy.wait()
 
@@ -499,24 +496,20 @@
     smem = pl.BlockSpec(memory_space=pltpu.SMEM)
     vmem = pl.BlockSpec(memory_space=pltpu.VMEM)
     anywhere = pl.BlockSpec(memory_space=pl.ANY)
-    (mine,) = call(
+    mine, edge_own, edge_other = pl.pallas_call(
         pack_kernel,
-        [((PIECE, 2 * D), bf16)],
-        [random_blocks, key_rows, value_rows],
-        56,
-        scalars=1,
-        bytes_accessed=1 << 19,
-    )
-    partner = permute(mine, ACROSS)
-    edge_own, edge_other = pl.pallas_call(
-        edge_kernel,
-        out_shape=[jax.ShapeDtypeStruct((B, 8 * D), bf16)] * 2,
-        in_specs=[smem, anywhere, anywhere, anywhere],
-        out_specs=[vmem, vmem],
+        out_shape=[
+            jax.ShapeDtypeStruct((PIECE, 2 * D), bf16),
+            jax.ShapeDtypeStruct((B, 8 * D), bf16),
+            jax.ShapeDtypeStruct((B, 8 * D), bf16),
+        ],
+        in_specs=[smem, vmem, vmem, anywhere, anywhere],
+        out_specs=[vmem, vmem, vmem],
         scratch_shapes=[pltpu.SemaphoreType.DMA((2, 2))],
         compiler_params=pltpu.CompilerParams(vmem_limit_bytes=56 * MIB),
-        cost_estimate=pl.CostEstimate(flops=0, bytes_accessed=1 << 27, transcendentals=0),
-    )(info, query_rows, out_grad, mine)
+        cost_estimate=pl.CostEstimate(flops=0, bytes_accessed=2 << 20, transcendentals=0),
+    )(random_blocks, key_rows, value_rows, query_rows, out_grad)
+    partner = permute(mine, ACROSS)
 
     edge = jnp.where(is_root, edge_own, jnp.zeros_like(edge_own))
     edge = edge + permute(edge_other, from_edge(0, 1))

time: 193 us -> 190 us (0.984)
    pallas_call x4 -> x3, Pallas kernels: 8.21 us -> 6.43 us  [call(): pl.pallas_call(kernel, out_shape=[jax.ShapeDtypeStruct(shape, dtype) for...]
where the time goes in v3:
time: 190 us; the launch traced here: 188 us
  waiting for transfers between devices  63.5 us (33%)
  starting transfers between devices  54.2 us (29%)
  Pallas kernels  33.8 us (18%)
  between operations  14.4 us (8%)
  blocking collectives  14 us (7%)
  other arithmetic  7.42 us (4%)
    ppermute x15, starting transfers between devices, permute(): return lax.ppermute(value, 'seq', pairs)  43.6 us
    all_to_all x1, waiting for transfers between devices, local(): recv = lax.all_to_all(send, 'seq', 0, 0)  42.7 us
    pallas_call x1, Pallas kernels, middle_call(): pl.pallas_call(middle_kernel, grid=(QB,), out_shape=[jax.ShapeDtypeStruct...  23.8 us
    ppermute x15, waiting for transfers between devices, permute(): return lax.ppermute(value, 'seq', pairs)  19.1 us
    all_to_all x1, blocking collectives, local(): lax.all_to_all(jnp.broadcast_to(stats, (ZN, *stats.shape)), 'seq', 0, 0,...  14 us
    all_to_all x1, starting transfers between devices, local(): recv = lax.all_to_all(send, 'seq', 0, 0)  10.5 us
    pallas_call x3, Pallas kernels, call(): pl.pallas_call(kernel, out_shape=[jax.ShapeDtypeStruct(shape, dtype) for...  6.43 us
  transfers between devices with their start and end apart: 17, of which 5 were waited for; matrix products, arithmetic and copies ran while one was open for 3% of the time, Pallas kernels for 15%

profile of v3, /device:TPU:1, one launch (start us, length us, event | category | flops | bytes accessed | tf_op | source)
XLA Modules:
  0.0 188.1 jit_solution(11711020827279765774)
XLA Ops:
  7.2 0.0 all-gather.2.cloned.1.call-start
  7.2 3.0 %shard_map.84 = (bf16[528,256]{1,0:T(8,128)(2,1)}, bf16[128,1024]{1,0:T(8,128)(2,1)}, bf16[128,1024]{1,0:T(8,128)(2,1)}) custom-call(s32[4,3]{1,0:T(4,128)} %ids_ref.1, bf16[512,128]{1,0:T(8,128)(2,1)} %k_ref.1, bf16[512,128]{1,0:T(8,128)(2,1)} %v_ref.1, bf16[512,1024]{1,0:T(8,128)(2,1)} %q_ref.3, bf16[512,1024]{1,0:T(8,128)(2,1)} %g_ref.3), custom_call_target="tpu_custom_call" | custom-call | bytes 2097152 | tf_op jit(solution)/shard_map/pallas_call | solution.py:499
  10.2 0.7 collective-permute-start.2
  10.9 0.7 collective-permute-start.3
  11.6 0.7 collective-permute-start.1
  12.3 3.7 %collective-permute-start = (bf16[528,256]{1,0:T(8,128)(2,1)}, bf16[528,256]{1,0:T(8,128)(2,1)S(1)}, u32[]{:S(2)}, u32[]{:S(2)}) collective-permute-start(bf16[528,256]{1,0:T(8,128)(2,1)} %get-tuple-element.27), channel_id=1, source_target_pairs={{0,128},{8,136},{16,144},{24,152},{32,160},{40,168},{48,176},{56,1... | collective-permute-start | bytes 811016 | tf_op jit(solution)/shard_map/ppermute | solution.py:79
  16.0 0.0 collective-permute-done.3
  16.0 0.1 add_add_fusion
  16.0 4.0 %collective-permute-done = bf16[528,256]{1,0:T(8,128)(2,1)S(1)} collective-permute-done((bf16[528,256]{1,0:T(8,128)(2,1)}, bf16[528,256]{1,0:T(8,128)(2,1)S(1)}, u32[]{:S(2)}, u32[]{:S(2)}) %collective-permute-start) | collective-permute-done | bytes 270368 | tf_op jit(solution)/shard_map/ppermute | solution.py:79
  20.0 1.8 pad_maximum_fusion.both_ref
  21.8 0.0 all-gather.2.cloned.1.call-update
  21.8 13.7 %collective-permute-start.6 = (bf16[1056,256]{1,0:T(8,128)(2,1)}, bf16[1056,256]{1,0:T(8,128)(2,1)S(1)}, u32[]{:S(2)}, u32[]{:S(2)}) collective-permute-start(bf16[1056,256]{1,0:T(8,128)(2,1)} %pad_maximum_fusion.both_ref), channel_id=1, source_target_pairs={{0,8},{8,0},{16,24},{24,16},{32,40},{40,32},{48,56},{56,48},{64,72... | collective-permute-start | bytes 1622024 | tf_op jit(solution)/shard_map/ppermute | solution.py:79
  35.5 0.7 collective-permute-start.4
  36.2 0.1 add.65
  36.2 1.3 collective-permute-start.5
  37.5 6.9 %collective-permute-done.5 = bf16[128,1024]{1,0:T(8,128)(2,1)S(1)} collective-permute-done((bf16[128,1024]{1,0:T(8,128)(2,1)S(1)}, bf16[128,1024]{1,0:T(8,128)(2,1)S(1)}, u32[]{:S(2)}, u32[]{:S(2)}) %collective-permute-start.5) | collective-permute-done | bytes 262176 | tf_op jit(solution)/shard_map/ppermute | solution.py:79
  44.5 0.1 add.66.edge_ref
  44.6 1.6 shard_map.85
  46.2 14.0 %all_to_all.10.stats_ref = f32[8,8,512]{2,1,0:T(8,128)S(1)} all-to-all(f32[8,8,512]{2,1,0:T(8,128)S(1)} %broadcast_in_dim.48), channel_id=1, replica_groups={{0,16,32,48,64,80,96,112},{8,24,40,56,72,88,104,120},{128,144,160,176,1..., dimensions={0} | all-to-all | bytes 262144 | tf_op jit(solution)/shard_map/all_to_all | solution.py:534
  60.2 3.0 %shard_map.86 = (bf16[128,1024]{1,0:T(8,128)(2,1)S(1)}, f32[512,256]{1,0:T(8,128)S(1)}, bf16[2,512,256]{2,1,0:T(8,128)(2,1)S(1)}, f32[512,256]{1,0:T(8,128)S(1)}) custom-call(bf16[128,1024]{1,0:T(8,128)(2,1)S(1)} %add.66.edge_ref, bf16[1056,256]{1,0:T(8,128)(2,1)S(1)} %copy-done, bf16[1056,256]{1,0:T(8,128)(2,1)S(1)} %collective-permute-done.6.other_ref, ...), custom_call_target="tpu_custom_call" | custom-call | flops 1610612736 | bytes 4194304 | tf_op jit(solution)/shard_map/pallas_call | solution.py:469
  63.2 10.3 %collective-permute-start.11 = (bf16[2,512,256]{2,1,0:T(8,128)(2,1)S(1)}, bf16[2,512,256]{2,1,0:T(8,128)(2,1)S(1)}, u32[]{:S(2)}, u32[]{:S(2)}) collective-permute-start(bf16[2,512,256]{2,1,0:T(8,128)(2,1)S(1)} %get-tuple-element.34), channel_id=1, source_target_pairs={{0,8},{8,0},{16,24},{24,16},{32,40},{40,32},{48,56},{56,48},{64,72... | collective-permute-start | bytes 1572872 | tf_op jit(solution)/shard_map/ppermute | solution.py:79
  73.5 2.2 %collective-permute-start.7 = (bf16[128,1024]{1,0:T(8,128)(2,1)S(1)}, bf16[128,1024]{1,0:T(8,128)(2,1)S(1)}, u32[]{:S(2)}, u32[]{:S(2)}) collective-permute-start(bf16[128,1024]{1,0:T(8,128)(2,1)S(1)} %get-tuple-element.32), channel_id=1, source_target_pairs={{16,0},{48,32},{80,64},{112,96},{104,120},{72,88},{40,56},{8,24},{... | collective-permute-start | bytes 786440 | tf_op jit(solution)/shard_map/ppermute | solution.py:79
  75.7 0.1 reshape.80
  75.8 0.6 pad_add_fusion.info
  76.4 8.2 %collective-permute-done.7 = bf16[128,1024]{1,0:T(8,128)(2,1)S(1)} collective-permute-done((bf16[128,1024]{1,0:T(8,128)(2,1)S(1)}, bf16[128,1024]{1,0:T(8,128)(2,1)S(1)}, u32[]{:S(2)}, u32[]{:S(2)}) %collective-permute-start.7) | collective-permute-done | bytes 262176 | tf_op jit(solution)/shard_map/ppermute | solution.py:79
  84.6 0.1 fusion.2._
  84.6 0.7 collective-permute-start.10
  85.3 1.4 collective-permute-start.9
  86.7 1.4 collective-permute-start.8
  88.1 0.1 fusion.1
  88.1 3.6 %collective-permute-start.12 = (bf16[512,256]{1,0:T(8,128)(2,1)S(1)}, bf16[512,256]{1,0:T(8,128)(2,1)S(1)}, u32[]{:S(2)}, u32[]{:S(2)}) collective-permute-start(bf16[512,256]{1,0:T(8,128)(2,1)S(1)} %fusion.1), channel_id=1, source_target_pairs={{0,128},{8,136},{16,144},{24,152},{32,160},{40,168},{48,176},{56,1... | collective-permute-start | bytes 786440 | tf_op jit(solution)/shard_map/ppermute | solution.py:79
  91.7 1.7 all-gather.2.cloned.1.call-done.all_ref
  93.4 23.8 %shard_map.87 = (bf16[512,1024]{1,0:T(8,128)(2,1)}, bf16[512,1024]{1,0:T(8,128)(2,1)}, bf16[32,128,256]{2,1,0:T(8,128)(2,1)}, f32[768,256]{1,0:T(8,128)}, bf16[128,256]{1,0:T(8,128)(2,1)}) custom-call(s32[16]{0:T(128)} %pad_add_fusion.info, bf16[512,1024]{1,0:T(8,128)(2,1)} %q_ref.3, bf16[512,1024]{1,0:T(8,128)(2,1)} %g_ref.3, ...), custom_call_target="tpu_custom_call" | custom-call | flops 6442450944 | bytes 16777216 | tf_op jit(solution)/shard_map/pallas_call | solution.py:410
  117.3 0.0 copy-start.6
  117.3 0.7 copy-done.4
  118.0 10.5 %all-to-all-start.1 = ((bf16[32,128,256]{2,1,0:T(8,128)(2,1)}), bf16[32,128,256]{2,1,0:T(8,128)(2,1)S(1)}, u32[]{:S(2)}, u32[]{:S(2)}) async-start(bf16[32,128,256]{2,1,0:T(8,128)(2,1)} %get-tuple-element.47), calls=%async_computation.1 | async-start | bytes 4194304 | tf_op jit(solution)/shard_map/all_to_all | solution.py:568
  128.6 2.1 %collective-permute-start.14 = (bf16[128,256]{1,0:T(8,128)(2,1)S(1)}, bf16[128,256]{1,0:T(8,128)(2,1)S(1)}, u32[]{:S(2)}, u32[]{:S(2)}) collective-permute-start(bf16[128,256]{1,0:T(8,128)(2,1)S(1)} %copy-done.6), channel_id=1, source_target_pairs={{8,0},{240,248},{9,1},{241,249},{10,2},{242,250},{11,3},{243,251},... | collective-permute-start | bytes 196616 | tf_op jit(solution)/shard_map/ppermute | solution.py:79
  130.7 1.2 add_convert_fusion
  132.0 0.7 collective-permute-start.13
  132.7 0.9 broadcast_and_fusion
  133.5 0.9 slice_convert_fusion
  134.4 0.2 select_reduce_fusion.1
  134.6 0.1 select_reduce_fusion
  134.7 0.1 pad_add_fusion.1.target
  134.8 1.3 fusion.base_ref
  136.2 0.6 shard_map.88
  136.8 42.7 %all-to-all-done.1.recv_ref = bf16[32,128,256]{2,1,0:T(8,128)(2,1)S(1)} async-done(((bf16[32,128,256]{2,1,0:T(8,128)(2,1)}), bf16[32,128,256]{2,1,0:T(8,128)(2,1)S(1)}, u32[]{:S(2)}, u32[]{:S(2)}) %all-to-all-start.1) | async-done | bytes 2097184 | tf_op jit(solution)/shard_map/all_to_all | solution.py:568
  179.4 1.9 shard_map.89
  (29 shorter events, 0.1 us)
Async XLA Ops:
  7.2 86.3 %all-gather.2.cloned.1.call-start = ((), (), s32[]{:S(2)}) async-start(), calls=%async_computation.2 | async-start | bytes 9191424 | tf_op jit(solution)/shard_map/all_gather | solution.py:519
  10.2 5.7 %collective-permute-start.2 = (bf16[128,1024]{1,0:T(8,128)(2,1)}, bf16[128,1024]{1,0:T(8,128)(2,1)S(1)}, u32[]{:S(2)}, u32[]{:S(2)}) collective-permute-start(bf16[128,1024]{1,0:T(8,128)(2,1)} %get-tuple-element.28), channel_id=1, source_target_pairs={{0,64},{248,184},{1,65},{249,185},{2,66},{250,186},{3,67},{251,187... | collective-permute-start | bytes 786440 | tf_op jit(solution)/shard_map/ppermute | solution.py:79
  10.9 5.0 %collective-permute-start.3 = (bf16[128,1024]{1,0:T(8,128)(2,1)}, bf16[128,1024]{1,0:T(8,128)(2,1)S(1)}, u32[]{:S(2)}, u32[]{:S(2)}) collective-permute-start(bf16[128,1024]{1,0:T(8,128)(2,1)} %get-tuple-element.29), channel_id=1, source_target_pairs={{0,192},{248,56},{1,193},{249,57},{2,194},{250,58},{3,195},{251,59... | collective-permute-start | bytes 786440 | tf_op jit(solution)/shard_map/ppermute | solution.py:79
  11.6 4.4 %collective-permute-start.1 = (bf16[128,1024]{1,0:T(8,128)(2,1)}, bf16[128,1024]{1,0:T(8,128)(2,1)S(1)}, u32[]{:S(2)}, u32[]{:S(2)}) collective-permute-start(bf16[128,1024]{1,0:T(8,128)(2,1)} %get-tuple-element.29), channel_id=1, source_target_pairs={{0,128},{248,120},{1,129},{249,121},{2,130},{250,122},{3,131},{251... | collective-permute-start | bytes 786440 | tf_op jit(solution)/shard_map/ppermute | solution.py:79
  12.3 7.7 %collective-permute-start = (bf16[528,256]{1,0:T(8,128)(2,1)}, bf16[528,256]{1,0:T(8,128)(2,1)S(1)}, u32[]{:S(2)}, u32[]{:S(2)}) collective-permute-start(bf16[528,256]{1,0:T(8,128)(2,1)} %get-tuple-element.27), channel_id=1, source_target_pairs={{0,128},{8,136},{16,144},{24,152},{32,160},{40,168},{48,176},{56,1... | collective-permute-start | bytes 811016 | tf_op jit(solution)/shard_map/ppermute | solution.py:79
  21.8 22.8 %copy-start = (bf16[1056,256]{1,0:T(8,128)(2,1)S(1)}, bf16[1056,256]{1,0:T(8,128)(2,1)}, u32[]{:S(2)}) copy-start(bf16[1056,256]{1,0:T(8,128)(2,1)} %pad_maximum_fusion.both_ref) | copy-start | bytes 1622020
  21.8 22.7 %collective-permute-start.6 = (bf16[1056,256]{1,0:T(8,128)(2,1)}, bf16[1056,256]{1,0:T(8,128)(2,1)S(1)}, u32[]{:S(2)}, u32[]{:S(2)}) collective-permute-start(bf16[1056,256]{1,0:T(8,128)(2,1)} %pad_maximum_fusion.both_ref), channel_id=1, source_target_pairs={{0,8},{8,0},{16,24},{24,16},{32,40},{40,32},{48,56},{56,48},{64,72... | collective-permute-start | bytes 1622024 | tf_op jit(solution)/shard_map/ppermute | solution.py:79
  35.5 0.7 collective-permute-start.4
  36.2 8.2 %collective-permute-start.5 = (bf16[128,1024]{1,0:T(8,128)(2,1)S(1)}, bf16[128,1024]{1,0:T(8,128)(2,1)S(1)}, u32[]{:S(2)}, u32[]{:S(2)}) collective-permute-start(bf16[128,1024]{1,0:T(8,128)(2,1)S(1)} %add.65), channel_id=1, source_target_pairs={{0,16},{32,48},{64,80},{96,112},{120,104},{88,72},{56,40},{24,8},{... | collective-permute-start | bytes 786440 | tf_op jit(solution)/shard_map/ppermute | solution.py:79
  60.2 15.5 %copy-start.5 = (s32[4,3]{1,0:T(4,128)S(1)}, s32[4,3]{1,0:T(4,128)}, u32[]{:S(2)}) copy-start(s32[4,3]{1,0:T(4,128)} %ids_ref.1) | copy-start | bytes 148
  63.2 24.9 %collective-permute-start.11 = (bf16[2,512,256]{2,1,0:T(8,128)(2,1)S(1)}, bf16[2,512,256]{2,1,0:T(8,128)(2,1)S(1)}, u32[]{:S(2)}, u32[]{:S(2)}) collective-permute-start(bf16[2,512,256]{2,1,0:T(8,128)(2,1)S(1)} %get-tuple-element.34), channel_id=1, source_target_pairs={{0,8},{8,0},{16,24},{24,16},{32,40},{40,32},{48,56},{56,48},{64,72... | collective-permute-start | bytes 1572872 | tf_op jit(solution)/shard_map/ppermute | solution.py:79
  73.5 11.0 %collective-permute-start.7 = (bf16[128,1024]{1,0:T(8,128)(2,1)S(1)}, bf16[128,1024]{1,0:T(8,128)(2,1)S(1)}, u32[]{:S(2)}, u32[]{:S(2)}) collective-permute-start(bf16[128,1024]{1,0:T(8,128)(2,1)S(1)} %get-tuple-element.32), channel_id=1, source_target_pairs={{16,0},{48,32},{80,64},{112,96},{104,120},{72,88},{40,56},{8,24},{... | collective-permute-start | bytes 786440 | tf_op jit(solution)/shard_map/ppermute | solution.py:79
  84.6 8.8 %copy-start.3 = (bf16[128,1024]{1,0:T(8,128)(2,1)}, bf16[128,1024]{1,0:T(8,128)(2,1)S(1)}, u32[]{:S(2)}) copy-start(bf16[128,1024]{1,0:T(8,128)(2,1)S(1)} %fusion.2._) | copy-start | bytes 786436
  84.6 32.6 %collective-permute-start.10 = (bf16[128,1024]{1,0:T(8,128)(2,1)S(1)}, bf16[128,1024]{1,0:T(8,128)(2,1)S(1)}, u32[]{:S(2)}, u32[]{:S(2)}) collective-permute-start(bf16[128,1024]{1,0:T(8,128)(2,1)S(1)} %fusion.2._), channel_id=1, source_target_pairs={{32,0},{88,120},{160,128},{216,248},{33,1},{89,121},{161,129},{217... | collective-permute-start | bytes 786440 | tf_op jit(solution)/shard_map/ppermute | solution.py:79
  85.3 31.9 %collective-permute-start.9 = (bf16[128,1024]{1,0:T(8,128)(2,1)S(1)}, bf16[128,1024]{1,0:T(8,128)(2,1)}, u32[]{:S(2)}, u32[]{:S(2)}) collective-permute-start(bf16[128,1024]{1,0:T(8,128)(2,1)S(1)} %fusion.2._), channel_id=1, source_target_pairs={{96,0},{24,120},{224,128},{152,248},{97,1},{25,121},{225,129},{153... | collective-permute-start | bytes 786440 | tf_op jit(solution)/shard_map/ppermute | solution.py:79
  86.7 30.5 %collective-permute-start.8 = (bf16[128,1024]{1,0:T(8,128)(2,1)S(1)}, bf16[128,1024]{1,0:T(8,128)(2,1)}, u32[]{:S(2)}, u32[]{:S(2)}) collective-permute-start(bf16[128,1024]{1,0:T(8,128)(2,1)S(1)} %fusion.2._), channel_id=1, source_target_pairs={{64,0},{56,120},{192,128},{184,248},{65,1},{57,121},{193,129},{185... | collective-permute-start | bytes 786440 | tf_op jit(solution)/shard_map/ppermute | solution.py:79
  88.1 29.1 %copy-start.2 = (bf16[2,512,256]{2,1,0:T(8,128)(2,1)}, bf16[2,512,256]{2,1,0:T(8,128)(2,1)S(1)}, u32[]{:S(2)}) copy-start(bf16[2,512,256]{2,1,0:T(8,128)(2,1)S(1)} %collective-permute-done.11) | copy-start | bytes 1572868
  88.1 29.1 %collective-permute-start.12 = (bf16[512,256]{1,0:T(8,128)(2,1)S(1)}, bf16[512,256]{1,0:T(8,128)(2,1)S(1)}, u32[]{:S(2)}, u32[]{:S(2)}) collective-permute-start(bf16[512,256]{1,0:T(8,128)(2,1)S(1)} %fusion.1), channel_id=1, source_target_pairs={{0,128},{8,136},{16,144},{24,152},{32,160},{40,168},{48,176},{56,1... | collective-permute-start | bytes 786440 | tf_op jit(solution)/shard_map/ppermute | solution.py:79
  117.3 0.7 copy-start.4
  117.3 11.3 %copy-start.6 = (bf16[128,256]{1,0:T(8,128)(2,1)S(1)}, bf16[128,256]{1,0:T(8,128)(2,1)}, u32[]{:S(2)}) copy-start(bf16[128,256]{1,0:T(8,128)(2,1)} %get-tuple-element.43) | copy-start | bytes 196612
  118.0 61.5 %all-to-all-start.1 = ((bf16[32,128,256]{2,1,0:T(8,128)(2,1)}), bf16[32,128,256]{2,1,0:T(8,128)(2,1)S(1)}, u32[]{:S(2)}, u32[]{:S(2)}) async-start(bf16[32,128,256]{2,1,0:T(8,128)(2,1)} %get-tuple-element.47), calls=%async_computation.1 | async-start | bytes 4194304 | tf_op jit(solution)/shard_map/all_to_all | solution.py:568
  128.6 7.6 %copy-start.1 = (s32[16]{0:T(128)S(1)}, s32[16]{0:T(128)}, u32[]{:S(2)}) copy-start(s32[16]{0:T(128)} %pad_add_fusion.info) | copy-start | bytes 196
  128.6 8.2 %collective-permute-start.14 = (bf16[128,256]{1,0:T(8,128)(2,1)S(1)}, bf16[128,256]{1,0:T(8,128)(2,1)S(1)}, u32[]{:S(2)}, u32[]{:S(2)}) collective-permute-start(bf16[128,256]{1,0:T(8,128)(2,1)S(1)} %copy-done.6), channel_id=1, source_target_pairs={{8,0},{240,248},{9,1},{241,249},{10,2},{242,250},{11,3},{243,251},... | collective-permute-start | bytes 196616 | tf_op jit(solution)/shard_map/ppermute | solution.py:79
  132.0 4.1 %collective-permute-start.13 = (bf16[128,1024]{1,0:T(8,128)(2,1)S(1)}, bf16[128,1024]{1,0:T(8,128)(2,1)S(1)}, u32[]{:S(2)}, u32[]{:S(2)}) collective-permute-start(bf16[128,1024]{1,0:T(8,128)(2,1)S(1)} %add_convert_fusion), channel_id=1, source_target_pairs={{128,0},{120,248},{129,1},{121,249},{130,2},{122,250},{131,3},{123... | collective-permute-start | bytes 786440 | tf_op jit(solution)/shard_map/ppermute | solution.py:79
Sparse Core Ops, SparseCore 0:
  21.9 71.4 all-gather.1

commit v4 on v3

--- a/solution.py
+++ b/solution.py
@@ -218,15 +218,18 @@
     out_ref, dq_ref, send_ref, state_ref, side_ref = refs[:5]
     kv, s_ref, e_all, ds_all, slots, sems, slot_sems = refs[5:]
     me = info[12]
-    j = pl.program_id(0)
-    last_step = j == QB - 1
-
-    def fetch(block, buffer, slot):
+    step = pl.program_id(0)
+    last_step = step == QB // 2 - 1
+    buffer = step & 1
+
+    def fetch(block, at, half, slot):
         block = jnp.clip(block, 0, NB - 1)
         place = place_of(block >> 2, me >> 4)
         row = pl.multiple_of(place * PIECE + (block & 3) * B, 16)
         return pltpu.make_async_copy(
-            all_ref.at[pl.ds(row, B), :], kv.at[buffer, pl.ds(slot * B, B), :], sems.at[buffer, slot]
+            all_ref.at[pl.ds(row, B), :],
+            kv.at[at, half, pl.ds(slot * B, B), :],
+            sems.at[at, half, slot],
         )
 
     def slot_copy(at, which, destination):
@@ -234,49 +237,44 @@
             slots.at[at, which], send_ref.at[destination], slot_sems.at[at, which]
         )
 
-    def fetch_all(step, buffer):
-        block = me * QB + step
-        for slot, name in enumerate((block - 1, block, block + 1, 0, NB - 1)):
-            fetch(jnp.int32(name), buffer, slot).start()
-        for r in range(3):
-            fetch(info[step * 3 + r], buffer, 5 + r).start()
-
-    @pl.when(j == 0)
+    def fetch_all(first, at):
+        for half in range(2):
+            block = me * QB + first + half
+            for slot, name in enumerate((block - 1, block, block + 1, 0, NB - 1)):
+                fetch(jnp.int32(name), at, half, slot).start()
+            for r in range(3):
+                fetch(info[(first + half) * 3 + r], at, half, 5 + r).start()
+
+    @pl.when(step == 0)
     def _():
         fetch_all(0, 0)
         state_ref[...] = jnp.zeros_like(state_ref)
         side_ref[...] = jnp.zeros_like(side_ref)
 
-    buffer = j & 1
-
     @pl.when(jnp.logical_not(last_step))
     def _():
-        fetch_all(j + 1, 1 - buffer)
-
-    for slot in range(SLOTS):
-        fetch(jnp.int32(0), buffer, slot).wait()
-
-    block = me * QB + j
-    middle = jnp.logical_and(block > 0, block < NB - 1)
-    to_low = jnp.logical_and(jnp.logical_and(middle, j == 0), me != 1)
-    to_high = jnp.logical_and(jnp.logical_and(middle, j == QB - 1), me != SEQ - 2)
-
-    @pl.when(middle)
-    def _():
+        fetch_all(2, 1)
+
+    for half in range(2):
+        for slot in range(SLOTS):
+            fetch(jnp.int32(0), buffer, half, slot).wait()
+
+    pairs = range(HEADS // 2)
+    heads = [[slice((2 * p + h) * D, (2 * p + h + 1) * D) for h in range(2)] for p in pairs]
+    chunks = [slice(n * B, (n + 1) * B) for n in range(KEYS // B)]
+
+    def work(half):
+        block = me * QB + 2 * step + half
         low_bias = jnp.where(block == 1, FAR, 0.0).astype(jnp.float32)
         high_bias = jnp.where(block == NB - 2, FAR, 0.0).astype(jnp.float32)
-        values_t = kv[buffer, :, D:].T
-        keys_t = kv[buffer, :, :D].T
+        rows = slice(half * B, (half + 1) * B)
         scaled_q, scaled_g = [], []
-        pairs = range(HEADS // 2)
-        heads = [[slice((2 * p + h) * D, (2 * p + h + 1) * D) for h in range(2)] for p in pairs]
-        chunks = [slice(n * B, (n + 1) * B) for n in range(KEYS // B)]
 
         def scores(pair):
-            q_t = jnp.concatenate([q_ref[:, h].T for h in heads[pair]], axis=1)
+            q_t = jnp.concatenate([q_ref[rows, h].T for h in heads[pair]], axis=1)
             top = None
             for n, c in enumerate(chunks):
-                s = dot(kv[buffer, c, :D], q_t)
+                s = dot(kv[buffer, half, c, :D], q_t)
                 if n == 0:
                     s = s + low_bias
                 if n == 2:
@@ -291,36 +289,58 @@
             total = None
             for c in chunks:
                 e = jnp.exp2(s_ref[pair % 2, c, :] * (SCALE * LOG2E) - top)
-                e_all[c, cols] = e.astype(jnp.bfloat16)
+                e_all[half, c, cols] = e.astype(jnp.bfloat16)
                 t = e.sum(axis=0, keepdims=True)
                 total = t if total is None else total + t
             return 1.0 / total
 
         def gradients(pair, part):
             cols = slice(pair * 2 * D, (pair + 1) * 2 * D)
-            g_t = jnp.concatenate([g_ref[:, h].T for h in heads[pair]], axis=1)
-            o = dot(values_t, e_all[:, cols]) * part
+            g_t = jnp.concatenate([g_ref[rows, h].T for h in heads[pair]], axis=1)
+            o = dot(values_t, e_all[half, :, cols]) * part
             delta = (g_t.astype(jnp.float32) * o).sum(axis=0, keepdims=True)
             for c in chunks:
-                e = e_all[c, cols].astype(jnp.float32)
-                ds_all[c, cols] = (e * (dot(kv[buffer, c, D:], g_t) - delta)).astype(jnp.bfloat16)
-            dq = dot(keys_t, ds_all[:, cols]) * (part * SCALE)
+                e = e_all[half, c, cols].astype(jnp.float32)
+                ds = e * (dot(kv[buffer, half, c, D:], g_t) - delta)
+                ds_all[half, c, cols] = ds.astype(jnp.bfloat16)
+            dq = dot(keys_t, ds_all[half, :, cols]) * (part * SCALE)
             for n, h in enumerate(heads[pair]):
                 one = slice(n * B, (n + 1) * B)
-                out_ref[:, h] = o[:, one].T.astype(jnp.bfloat16)
-                dq_ref[:, h] = dq[:, one].T.astype(jnp.bfloat16)
+                out_ref[rows, h] = o[:, one].T.astype(jnp.bfloat16)
+                dq_ref[rows, h] = dq[:, one].T.astype(jnp.bfloat16)
                 column = part[:, one].T
-                scaled_q.append((q_ref[:, h] * (column * SCALE)).astype(jnp.bfloat16))
-                scaled_g.append((g_ref[:, h] * column).astype(jnp.bfloat16))
+                scaled_q.append((q_ref[rows, h] * (column * SCALE)).astype(jnp.bfloat16))
+                scaled_g.append((g_ref[rows, h] * column).astype(jnp.bfloat16))
 
         top = scores(0)
+        yield None
+        values_t = kv[buffer, half, :, D:].T
+        keys_t = kv[buffer, half, :, :D].T
         for pair in pairs:
             part = weights(pair, top)
             if pair + 1 < HEADS // 2:
                 top = scores(pair + 1)
             gradients(pair, part)
-        dk = dot(ds_all[...], jnp.concatenate(scaled_q, axis=0))
-        dv = dot(e_all[...], jnp.concatenate(scaled_g, axis=0))
+        yield None
+        dk = dot(ds_all[half], jnp.concatenate(scaled_q, axis=0))
+        dv = dot(e_all[half], jnp.concatenate(scaled_g, axis=0))
+        yield dk, dv
+
+    first, second = work(0), work(1)
+    next(first)
+    next(first)
+    next(second)
+    results = [next(first)]
+    next(second)
+    results.append(next(second))
+
+    def add(half):
+        j = 2 * step + half
+        block = me * QB + j
+        middle = jnp.logical_and(block > 0, block < NB - 1)
+        to_low = jnp.logical_and(jnp.logical_and(middle, j == 0), me != 1)
+        to_high = jnp.logical_and(jnp.logical_and(middle, j == QB - 1), me != SEQ - 2)
+        dk, dv = results[half]
 
         def contribution(slot):
             rows = slice(slot * B, (slot + 1) * B)
@@ -329,45 +349,61 @@
         def low(slot):
             return contribution(slot).astype(jnp.bfloat16)
 
-        state_ref[pl.ds(pl.multiple_of(j * B, B), B), :] += contribution(1)
-        state_ref[ROWS : ROWS + B, :] += contribution(3)
-        state_ref[ROWS + B :, :] += contribution(4)
-
-        @pl.when(j > 0)
+        @pl.when(middle)
         def _():
-            state_ref[pl.ds(pl.multiple_of((j - 1) * B, B), B), :] += contribution(0)
-
-        @pl.when(j < QB - 1)
-        def _():
-            state_ref[pl.ds(pl.multiple_of((j + 1) * B, B), B), :] += contribution(2)
-
-        for r in range(3):
-            slots[j, r] = low(5 + r)
-            slot_copy(j, r, info[j * 3 + r] >> 2).start()
-
-        @pl.when(j == 0)
-        def _():
-            slots[j, 3] = low(0)
-
-        @pl.when(j == QB - 1)
-        def _():
-            slots[j, 3] = low(2)
-
-        @pl.when(to_low)
-        def _():
-            slot_copy(j, 3, me - 1).start()
-
-        @pl.when(to_high)
-        def _():
-            slot_copy(j, 3, me + 1).start()
-
-        @pl.when(jnp.logical_and(j == 0, me == 1))
-        def _():
-            side_ref[...] = low(0)
-
-        @pl.when(jnp.logical_and(j == QB - 1, me == SEQ - 2))
-        def _():
-            side_ref[...] = low(2)
+            state_ref[pl.ds(pl.multiple_of(j * B, B), B), :] += contribution(1)
+            state_ref[ROWS : ROWS + B, :] += contribution(3)
+            state_ref[ROWS + B :, :] += contribution(4)
+
+            @pl.when(j > 0)
+            def _():
+                state_ref[pl.ds(pl.multiple_of((j - 1) * B, B), B), :] += contribution(0)
+
+            @pl.when(j < QB - 1)
+            def _():
+                state_ref[pl.ds(pl.multiple_of((j + 1) * B, B), B), :] += contribution(2)
+
+            for r in range(3):
+                slots[j, r] = low(5 + r)
+                slot_copy(j, r, info[j * 3 + r] >> 2).start()
+
+            @pl.when(j == 0)
+            def _():
+                slots[j, 3] = low(0)
+
+            @pl.when(j == QB - 1)
+            def _():
+                slots[j, 3] = low(2)
+
+            @pl.when(to_low)
+            def _():
+                slot_copy(j, 3, me - 1).start()
+
+            @pl.when(to_high)
+            def _():
+                slot_copy(j, 3, me + 1).start()
+
+            @pl.when(jnp.logical_and(j == 0, me == 1))
+            def _():
+                side_ref[...] = low(0)
+
+            @pl.when(jnp.logical_and(j == QB - 1, me == SEQ - 2))
+            def _():
+                side_ref[...] = low(2)
+
+        def finish():
+            @pl.when(middle)
+            def _():
+                for r in range(3):
+                    slot_copy(j, r, 0).wait()
+
+            @pl.when(jnp.logical_or(to_low, to_high))
+            def _():
+                slot_copy(j, 3, 0).wait()
+
+        return finish
+
+    finishes = [add(0), add(1)]
 
     @pl.when(last_step)
     def _():
@@ -392,24 +428,18 @@
             slot_copy(QB, 1, SEQ - 1).start()
             slot_copy(QB, 1, SEQ - 1).wait()
 
-    @pl.when(middle)
-    def _():
-        for r in range(3):
-            slot_copy(j, r, 0).wait()
-
-    @pl.when(jnp.logical_or(to_low, to_high))
-    def _():
-        slot_copy(j, 3, 0).wait()
+    for finish in finishes:
+        finish()
 
 
 def middle_call(info, query_rows, out_grad, gathered, later):
     bf16, f32 = jnp.bfloat16, jnp.float32
     anywhere = pl.BlockSpec(memory_space=pl.ANY)
     whole = pl.BlockSpec(memory_space=pltpu.VMEM)
-    rows = pl.BlockSpec((B, HEADS * D), lambda j: (j, 0))
+    rows = pl.BlockSpec((2 * B, HEADS * D), lambda step: (step, 0))
     return pl.pallas_call(
         middle_kernel,
-        grid=(QB,),
+        grid=(QB // 2,),
         out_shape=[
             jax.ShapeDtypeStruct((ROWS, HEADS * D), bf16),
             jax.ShapeDtypeStruct((ROWS, HEADS * D), bf16),
@@ -420,12 +450,12 @@
         in_specs=[pl.BlockSpec(memory_space=pltpu.SMEM), rows, rows, anywhere, anywhere],
         out_specs=[rows, rows, anywhere, whole, whole],
         scratch_shapes=[
-            pltpu.VMEM((2, KEYS, 2 * D), bf16),
+            pltpu.VMEM((2, 2, KEYS, 2 * D), bf16),
             pltpu.VMEM((2, KEYS, 2 * D), f32),
-            pltpu.VMEM((KEYS, HEADS * B), bf16),
-            pltpu.VMEM((KEYS, HEADS * B), bf16),
+            pltpu.VMEM((2, KEYS, HEADS * B), bf16),
+            pltpu.VMEM((2, KEYS, HEADS * B), bf16),
             pltpu.VMEM((QB + 1, 4, B, 2 * D), bf16),
-            pltpu.SemaphoreType.DMA((2, SLOTS)),
+            pltpu.SemaphoreType.DMA((2, 2, SLOTS)),
             pltpu.SemaphoreType.DMA((QB + 1, 4)),
         ],
         compiler_params=pltpu.CompilerParams(vmem_limit_bytes=56 * MIB),

time: 190 us -> 189 us (level)
  no operation moved by 1% of the time
where the time goes in v4:
time: 189 us; the launch traced here: 187 us
  waiting for transfers between devices  63.5 us (34%)
  starting transfers between devices  54.3 us (29%)
  Pallas kernels  32.9 us (17%)
  between operations  14.4 us (8%)
  blocking collectives  14 us (7%)
  other arithmetic  7.42 us (4%)
    ppermute x15, starting transfers between devices, permute(): return lax.ppermute(value, 'seq', pairs)  43.6 us
    all_to_all x1, waiting for transfers between devices, local(): recv = lax.all_to_all(send, 'seq', 0, 0)  42.7 us
    pallas_call x1, Pallas kernels, middle_call(): pl.pallas_call(middle_kernel, grid=(QB // 2,), out_shape=[jax.ShapeDtypeS...  22.9 us
    ppermute x15, waiting for transfers between devices, permute(): return lax.ppermute(value, 'seq', pairs)  19.1 us
    all_to_all x1, blocking collectives, local(): lax.all_to_all(jnp.broadcast_to(stats, (ZN, *stats.shape)), 'seq', 0, 0,...  14 us
    all_to_all x1, starting transfers between devices, local(): recv = lax.all_to_all(send, 'seq', 0, 0)  10.6 us
    pallas_call x3, Pallas kernels, call(): pl.pallas_call(kernel, out_shape=[jax.ShapeDtypeStruct(shape, dtype) for...  6.46 us
  transfers between devices with their start and end apart: 17, of which 5 were waited for; matrix products, arithmetic and copies ran while one was open for 3% of the time, Pallas kernels for 15%

profile of v4, /device:TPU:1, one launch (start us, length us, event | category | flops | bytes accessed | tf_op | source)
XLA Modules:
  0.0 187.4 jit_solution(11329347949617460491)
XLA Ops:
  7.2 0.0 all-gather.2.cloned.1.call-start
  7.2 3.0 %shard_map.84 = (bf16[528,256]{1,0:T(8,128)(2,1)}, bf16[128,1024]{1,0:T(8,128)(2,1)}, bf16[128,1024]{1,0:T(8,128)(2,1)}) custom-call(s32[4,3]{1,0:T(4,128)} %ids_ref.1, bf16[512,128]{1,0:T(8,128)(2,1)} %k_ref.1, bf16[512,128]{1,0:T(8,128)(2,1)} %v_ref.1, bf16[512,1024]{1,0:T(8,128)(2,1)} %q_ref.3, bf16[512,1024]{1,0:T(8,128)(2,1)} %g_ref.3), custom_call_target="tpu_custom_call" | custom-call | bytes 2097152 | tf_op jit(solution)/shard_map/pallas_call | solution.py:529
  10.2 0.7 collective-permute-start.2
  10.9 0.7 collective-permute-start.3
  11.6 0.7 collective-permute-start.1
  12.3 3.7 %collective-permute-start = (bf16[528,256]{1,0:T(8,128)(2,1)}, bf16[528,256]{1,0:T(8,128)(2,1)S(1)}, u32[]{:S(2)}, u32[]{:S(2)}) collective-permute-start(bf16[528,256]{1,0:T(8,128)(2,1)} %get-tuple-element.27), channel_id=1, source_target_pairs={{0,128},{8,136},{16,144},{24,152},{32,160},{40,168},{48,176},{56,1... | collective-permute-start | bytes 811016 | tf_op jit(solution)/shard_map/ppermute | solution.py:79
  16.0 0.0 collective-permute-done.2
  16.0 0.1 add_add_fusion
  16.0 4.0 %collective-permute-done = bf16[528,256]{1,0:T(8,128)(2,1)S(1)} collective-permute-done((bf16[528,256]{1,0:T(8,128)(2,1)}, bf16[528,256]{1,0:T(8,128)(2,1)S(1)}, u32[]{:S(2)}, u32[]{:S(2)}) %collective-permute-start) | collective-permute-done | bytes 270368 | tf_op jit(solution)/shard_map/ppermute | solution.py:79
  20.0 1.8 pad_maximum_fusion.both_ref
  21.8 0.0 all-gather.2.cloned.1.call-update
  21.8 13.7 %collective-permute-start.6 = (bf16[1056,256]{1,0:T(8,128)(2,1)}, bf16[1056,256]{1,0:T(8,128)(2,1)S(1)}, u32[]{:S(2)}, u32[]{:S(2)}) collective-permute-start(bf16[1056,256]{1,0:T(8,128)(2,1)} %pad_maximum_fusion.both_ref), channel_id=1, source_target_pairs={{0,8},{8,0},{16,24},{24,16},{32,40},{40,32},{48,56},{56,48},{64,72... | collective-permute-start | bytes 1622024 | tf_op jit(solution)/shard_map/ppermute | solution.py:79
  35.5 0.7 collective-permute-start.4
  36.2 0.1 add.65
  36.2 1.3 collective-permute-start.5
  37.5 6.9 %collective-permute-done.5 = bf16[128,1024]{1,0:T(8,128)(2,1)S(1)} collective-permute-done((bf16[128,1024]{1,0:T(8,128)(2,1)S(1)}, bf16[128,1024]{1,0:T(8,128)(2,1)S(1)}, u32[]{:S(2)}, u32[]{:S(2)}) %collective-permute-start.5) | collective-permute-done | bytes 262176 | tf_op jit(solution)/shard_map/ppermute | solution.py:79
  44.5 0.1 add.66.edge_ref
  44.6 1.6 shard_map.85
  46.2 14.0 %all_to_all.10.stats_ref = f32[8,8,512]{2,1,0:T(8,128)S(1)} all-to-all(f32[8,8,512]{2,1,0:T(8,128)S(1)} %broadcast_in_dim.48), channel_id=1, replica_groups={{0,16,32,48,64,80,96,112},{8,24,40,56,72,88,104,120},{128,144,160,176,1..., dimensions={0} | all-to-all | bytes 262144 | tf_op jit(solution)/shard_map/all_to_all | solution.py:564
  60.2 3.0 %shard_map.86 = (bf16[128,1024]{1,0:T(8,128)(2,1)S(1)}, f32[512,256]{1,0:T(8,128)S(1)}, bf16[2,512,256]{2,1,0:T(8,128)(2,1)S(1)}, f32[512,256]{1,0:T(8,128)S(1)}) custom-call(bf16[128,1024]{1,0:T(8,128)(2,1)S(1)} %add.66.edge_ref, bf16[1056,256]{1,0:T(8,128)(2,1)S(1)} %copy-done, bf16[1056,256]{1,0:T(8,128)(2,1)S(1)} %collective-permute-done.6.other_ref, ...), custom_call_target="tpu_custom_call" | custom-call | flops 1610612736 | bytes 4194304 | tf_op jit(solution)/shard_map/pallas_call | solution.py:499
  63.2 10.3 %collective-permute-start.11 = (bf16[2,512,256]{2,1,0:T(8,128)(2,1)S(1)}, bf16[2,512,256]{2,1,0:T(8,128)(2,1)S(1)}, u32[]{:S(2)}, u32[]{:S(2)}) collective-permute-start(bf16[2,512,256]{2,1,0:T(8,128)(2,1)S(1)} %get-tuple-element.34), channel_id=1, source_target_pairs={{0,8},{8,0},{16,24},{24,16},{32,40},{40,32},{48,56},{56,48},{64,72... | collective-permute-start | bytes 1572872 | tf_op jit(solution)/shard_map/ppermute | solution.py:79
  73.5 2.2 %collective-permute-start.7 = (bf16[128,1024]{1,0:T(8,128)(2,1)S(1)}, bf16[128,1024]{1,0:T(8,128)(2,1)S(1)}, u32[]{:S(2)}, u32[]{:S(2)}) collective-permute-start(bf16[128,1024]{1,0:T(8,128)(2,1)S(1)} %get-tuple-element.32), channel_id=1, source_target_pairs={{16,0},{48,32},{80,64},{112,96},{104,120},{72,88},{40,56},{8,24},{... | collective-permute-start | bytes 786440 | tf_op jit(solution)/shard_map/ppermute | solution.py:79
  75.7 0.1 reshape.80
  75.8 0.6 pad_add_fusion.info
  76.4 8.2 %collective-permute-done.7 = bf16[128,1024]{1,0:T(8,128)(2,1)S(1)} collective-permute-done((bf16[128,1024]{1,0:T(8,128)(2,1)S(1)}, bf16[128,1024]{1,0:T(8,128)(2,1)S(1)}, u32[]{:S(2)}, u32[]{:S(2)}) %collective-permute-start.7) | collective-permute-done | bytes 262176 | tf_op jit(solution)/shard_map/ppermute | solution.py:79
  84.6 0.1 fusion.2._
  84.6 0.7 collective-permute-start.10
  85.3 1.4 collective-permute-start.9
  86.7 1.4 collective-permute-start.8
  88.1 0.1 fusion.1
  88.1 3.6 %collective-permute-start.12 = (bf16[512,256]{1,0:T(8,128)(2,1)S(1)}, bf16[512,256]{1,0:T(8,128)(2,1)S(1)}, u32[]{:S(2)}, u32[]{:S(2)}) collective-permute-start(bf16[512,256]{1,0:T(8,128)(2,1)S(1)} %fusion.1), channel_id=1, source_target_pairs={{0,128},{8,136},{16,144},{24,152},{32,160},{40,168},{48,176},{56,1... | collective-permute-start | bytes 786440 | tf_op jit(solution)/shard_map/ppermute | solution.py:79
  91.7 1.7 all-gather.2.cloned.1.call-done.all_ref
  93.4 22.9 %shard_map.87 = (bf16[512,1024]{1,0:T(8,128)(2,1)}, bf16[512,1024]{1,0:T(8,128)(2,1)}, bf16[32,128,256]{2,1,0:T(8,128)(2,1)}, f32[768,256]{1,0:T(8,128)}, bf16[128,256]{1,0:T(8,128)(2,1)}) custom-call(s32[16]{0:T(128)} %pad_add_fusion.info, bf16[512,1024]{1,0:T(8,128)(2,1)} %q_ref.3, bf16[512,1024]{1,0:T(8,128)(2,1)} %g_ref.3, ...), custom_call_target="tpu_custom_call" | custom-call | flops 6442450944 | bytes 16777216 | tf_op jit(solution)/shard_map/pallas_call | solution.py:440
  116.4 0.0 copy-start.6
  116.4 0.7 copy-done.4
  117.1 10.6 %all-to-all-start.1 = ((bf16[32,128,256]{2,1,0:T(8,128)(2,1)}), bf16[32,128,256]{2,1,0:T(8,128)(2,1)S(1)}, u32[]{:S(2)}, u32[]{:S(2)}) async-start(bf16[32,128,256]{2,1,0:T(8,128)(2,1)} %get-tuple-element.47), calls=%async_computation.1 | async-start | bytes 4194304 | tf_op jit(solution)/shard_map/all_to_all | solution.py:598
  127.8 2.1 %collective-permute-start.14 = (bf16[128,256]{1,0:T(8,128)(2,1)S(1)}, bf16[128,256]{1,0:T(8,128)(2,1)S(1)}, u32[]{:S(2)}, u32[]{:S(2)}) collective-permute-start(bf16[128,256]{1,0:T(8,128)(2,1)S(1)} %copy-done.6), channel_id=1, source_target_pairs={{8,0},{240,248},{9,1},{241,249},{10,2},{242,250},{11,3},{243,251},... | collective-permute-start | bytes 196616 | tf_op jit(solution)/shard_map/ppermute | solution.py:79
  129.9 1.2 add_convert_fusion
  131.2 0.7 collective-permute-start.13
  131.9 0.9 broadcast_and_fusion
  132.7 0.9 slice_convert_fusion
  133.6 0.2 select_reduce_fusion.1
  133.8 0.1 select_reduce_fusion
  133.9 0.1 pad_add_fusion.1.target
  134.0 1.3 fusion.base_ref
  135.4 0.6 shard_map.88
  136.0 42.7 %all-to-all-done.1.recv_ref = bf16[32,128,256]{2,1,0:T(8,128)(2,1)S(1)} async-done(((bf16[32,128,256]{2,1,0:T(8,128)(2,1)}), bf16[32,128,256]{2,1,0:T(8,128)(2,1)S(1)}, u32[]{:S(2)}, u32[]{:S(2)}) %all-to-all-start.1) | async-done | bytes 2097184 | tf_op jit(solution)/shard_map/all_to_all | solution.py:598
  178.6 1.9 %shard_map.89 = (bf16[512,128]{1,0:T(8,128)(2,1)}, bf16[512,128]{1,0:T(8,128)(2,1)}) custom-call(s32[33]{0:T(128)S(1)} %pad_add_fusion.1.target, bf16[128,256]{1,0:T(8,128)(2,1)S(1)} %collective-permute-done.14.extra_ref, f32[512,256]{1,0:T(8,128)S(1)} %fusion.base_ref, bf16[32,128,256]{2,1,0:T(8,128)(2,1)S(1)} %all-to-all-done.1.recv_ref), custom_call_target="tpu_custom_call" | custom-call | flops 1048576 | bytes 4194304 | tf_op jit(solution)/shard_map/pallas_call | solution.py:499
  (29 shorter events, 0.1 us)
Async XLA Ops:
  7.2 86.3 %all-gather.2.cloned.1.call-start = ((), (), s32[]{:S(2)}) async-start(), calls=%async_computation.2 | async-start | bytes 9191424 | tf_op jit(solution)/shard_map/all_gather | solution.py:549
  10.2 5.7 %collective-permute-start.2 = (bf16[128,1024]{1,0:T(8,128)(2,1)}, bf16[128,1024]{1,0:T(8,128)(2,1)S(1)}, u32[]{:S(2)}, u32[]{:S(2)}) collective-permute-start(bf16[128,1024]{1,0:T(8,128)(2,1)} %get-tuple-element.28), channel_id=1, source_target_pairs={{0,64},{248,184},{1,65},{249,185},{2,66},{250,186},{3,67},{251,187... | collective-permute-start | bytes 786440 | tf_op jit(solution)/shard_map/ppermute | solution.py:79
  10.9 5.0 %collective-permute-start.3 = (bf16[128,1024]{1,0:T(8,128)(2,1)}, bf16[128,1024]{1,0:T(8,128)(2,1)S(1)}, u32[]{:S(2)}, u32[]{:S(2)}) collective-permute-start(bf16[128,1024]{1,0:T(8,128)(2,1)} %get-tuple-element.29), channel_id=1, source_target_pairs={{0,192},{248,56},{1,193},{249,57},{2,194},{250,58},{3,195},{251,59... | collective-permute-start | bytes 786440 | tf_op jit(solution)/shard_map/ppermute | solution.py:79
  11.6 4.4 %collective-permute-start.1 = (bf16[128,1024]{1,0:T(8,128)(2,1)}, bf16[128,1024]{1,0:T(8,128)(2,1)S(1)}, u32[]{:S(2)}, u32[]{:S(2)}) collective-permute-start(bf16[128,1024]{1,0:T(8,128)(2,1)} %get-tuple-element.29), channel_id=1, source_target_pairs={{0,128},{248,120},{1,129},{249,121},{2,130},{250,122},{3,131},{251... | collective-permute-start | bytes 786440 | tf_op jit(solution)/shard_map/ppermute | solution.py:79
  12.3 7.7 %collective-permute-start = (bf16[528,256]{1,0:T(8,128)(2,1)}, bf16[528,256]{1,0:T(8,128)(2,1)S(1)}, u32[]{:S(2)}, u32[]{:S(2)}) collective-permute-start(bf16[528,256]{1,0:T(8,128)(2,1)} %get-tuple-element.27), channel_id=1, source_target_pairs={{0,128},{8,136},{16,144},{24,152},{32,160},{40,168},{48,176},{56,1... | collective-permute-start | bytes 811016 | tf_op jit(solution)/shard_map/ppermute | solution.py:79
  21.8 22.8 %copy-start = (bf16[1056,256]{1,0:T(8,128)(2,1)S(1)}, bf16[1056,256]{1,0:T(8,128)(2,1)}, u32[]{:S(2)}) copy-start(bf16[1056,256]{1,0:T(8,128)(2,1)} %pad_maximum_fusion.both_ref) | copy-start | bytes 1622020
  21.8 22.7 %collective-permute-start.6 = (bf16[1056,256]{1,0:T(8,128)(2,1)}, bf16[1056,256]{1,0:T(8,128)(2,1)S(1)}, u32[]{:S(2)}, u32[]{:S(2)}) collective-permute-start(bf16[1056,256]{1,0:T(8,128)(2,1)} %pad_maximum_fusion.both_ref), channel_id=1, source_target_pairs={{0,8},{8,0},{16,24},{24,16},{32,40},{40,32},{48,56},{56,48},{64,72... | collective-permute-start | bytes 1622024 | tf_op jit(solution)/shard_map/ppermute | solution.py:79
  35.5 0.7 collective-permute-start.4
  36.2 8.2 %collective-permute-start.5 = (bf16[128,1024]{1,0:T(8,128)(2,1)S(1)}, bf16[128,1024]{1,0:T(8,128)(2,1)S(1)}, u32[]{:S(2)}, u32[]{:S(2)}) collective-permute-start(bf16[128,1024]{1,0:T(8,128)(2,1)S(1)} %add.65), channel_id=1, source_target_pairs={{0,16},{32,48},{64,80},{96,112},{120,104},{88,72},{56,40},{24,8},{... | collective-permute-start | bytes 786440 | tf_op jit(solution)/shard_map/ppermute | solution.py:79
  60.2 15.5 %copy-start.5 = (s32[4,3]{1,0:T(4,128)S(1)}, s32[4,3]{1,0:T(4,128)}, u32[]{:S(2)}) copy-start(s32[4,3]{1,0:T(4,128)} %ids_ref.1) | copy-start | bytes 148
  63.2 24.9 %collective-permute-start.11 = (bf16[2,512,256]{2,1,0:T(8,128)(2,1)S(1)}, bf16[2,512,256]{2,1,0:T(8,128)(2,1)S(1)}, u32[]{:S(2)}, u32[]{:S(2)}) collective-permute-start(bf16[2,512,256]{2,1,0:T(8,128)(2,1)S(1)} %get-tuple-element.34), channel_id=1, source_target_pairs={{0,8},{8,0},{16,24},{24,16},{32,40},{40,32},{48,56},{56,48},{64,72... | collective-permute-start | bytes 1572872 | tf_op jit(solution)/shard_map/ppermute | solution.py:79
  73.5 11.0 %collective-permute-start.7 = (bf16[128,1024]{1,0:T(8,128)(2,1)S(1)}, bf16[128,1024]{1,0:T(8,128)(2,1)S(1)}, u32[]{:S(2)}, u32[]{:S(2)}) collective-permute-start(bf16[128,1024]{1,0:T(8,128)(2,1)S(1)} %get-tuple-element.32), channel_id=1, source_target_pairs={{16,0},{48,32},{80,64},{112,96},{104,120},{72,88},{40,56},{8,24},{... | collective-permute-start | bytes 786440 | tf_op jit(solution)/shard_map/ppermute | solution.py:79
  84.6 8.8 %copy-start.3 = (bf16[128,1024]{1,0:T(8,128)(2,1)}, bf16[128,1024]{1,0:T(8,128)(2,1)S(1)}, u32[]{:S(2)}) copy-start(bf16[128,1024]{1,0:T(8,128)(2,1)S(1)} %fusion.2._) | copy-start | bytes 786436
  84.6 31.7 %collective-permute-start.10 = (bf16[128,1024]{1,0:T(8,128)(2,1)S(1)}, bf16[128,1024]{1,0:T(8,128)(2,1)S(1)}, u32[]{:S(2)}, u32[]{:S(2)}) collective-permute-start(bf16[128,1024]{1,0:T(8,128)(2,1)S(1)} %fusion.2._), channel_id=1, source_target_pairs={{32,0},{88,120},{160,128},{216,248},{33,1},{89,121},{161,129},{217... | collective-permute-start | bytes 786440 | tf_op jit(solution)/shard_map/ppermute | solution.py:79
  85.3 31.0 %collective-permute-start.9 = (bf16[128,1024]{1,0:T(8,128)(2,1)S(1)}, bf16[128,1024]{1,0:T(8,128)(2,1)}, u32[]{:S(2)}, u32[]{:S(2)}) collective-permute-start(bf16[128,1024]{1,0:T(8,128)(2,1)S(1)} %fusion.2._), channel_id=1, source_target_pairs={{96,0},{24,120},{224,128},{152,248},{97,1},{25,121},{225,129},{153... | collective-permute-start | bytes 786440 | tf_op jit(solution)/shard_map/ppermute | solution.py:79
  86.7 29.7 %collective-permute-start.8 = (bf16[128,1024]{1,0:T(8,128)(2,1)S(1)}, bf16[128,1024]{1,0:T(8,128)(2,1)}, u32[]{:S(2)}, u32[]{:S(2)}) collective-permute-start(bf16[128,1024]{1,0:T(8,128)(2,1)S(1)} %fusion.2._), channel_id=1, source_target_pairs={{64,0},{56,120},{192,128},{184,248},{65,1},{57,121},{193,129},{185... | collective-permute-start | bytes 786440 | tf_op jit(solution)/shard_map/ppermute | solution.py:79
  88.1 28.3 %copy-start.2 = (bf16[2,512,256]{2,1,0:T(8,128)(2,1)}, bf16[2,512,256]{2,1,0:T(8,128)(2,1)S(1)}, u32[]{:S(2)}) copy-start(bf16[2,512,256]{2,1,0:T(8,128)(2,1)S(1)} %collective-permute-done.11) | copy-start | bytes 1572868
  88.1 28.2 %collective-permute-start.12 = (bf16[512,256]{1,0:T(8,128)(2,1)S(1)}, bf16[512,256]{1,0:T(8,128)(2,1)S(1)}, u32[]{:S(2)}, u32[]{:S(2)}) collective-permute-start(bf16[512,256]{1,0:T(8,128)(2,1)S(1)} %fusion.1), channel_id=1, source_target_pairs={{0,128},{8,136},{16,144},{24,152},{32,160},{40,168},{48,176},{56,1... | collective-permute-start | bytes 786440 | tf_op jit(solution)/shard_map/ppermute | solution.py:79
  116.4 0.7 copy-start.4
  116.4 11.4 %copy-start.6 = (bf16[128,256]{1,0:T(8,128)(2,1)S(1)}, bf16[128,256]{1,0:T(8,128)(2,1)}, u32[]{:S(2)}) copy-start(bf16[128,256]{1,0:T(8,128)(2,1)} %get-tuple-element.43) | copy-start | bytes 196612
  117.1 61.6 %all-to-all-start.1 = ((bf16[32,128,256]{2,1,0:T(8,128)(2,1)}), bf16[32,128,256]{2,1,0:T(8,128)(2,1)S(1)}, u32[]{:S(2)}, u32[]{:S(2)}) async-start(bf16[32,128,256]{2,1,0:T(8,128)(2,1)} %get-tuple-element.47), calls=%async_computation.1 | async-start | bytes 4194304 | tf_op jit(solution)/shard_map/all_to_all | solution.py:598
  127.8 7.6 %copy-start.1 = (s32[16]{0:T(128)S(1)}, s32[16]{0:T(128)}, u32[]{:S(2)}) copy-start(s32[16]{0:T(128)} %pad_add_fusion.info) | copy-start | bytes 196
  127.8 8.2 %collective-permute-start.14 = (bf16[128,256]{1,0:T(8,128)(2,1)S(1)}, bf16[128,256]{1,0:T(8,128)(2,1)S(1)}, u32[]{:S(2)}, u32[]{:S(2)}) collective-permute-start(bf16[128,256]{1,0:T(8,128)(2,1)S(1)} %copy-done.6), channel_id=1, source_target_pairs={{8,0},{240,248},{9,1},{241,249},{10,2},{242,250},{11,3},{243,251},... | collective-permute-start | bytes 196616 | tf_op jit(solution)/shard_map/ppermute | solution.py:79
  131.2 4.1 %collective-permute-start.13 = (bf16[128,1024]{1,0:T(8,128)(2,1)S(1)}, bf16[128,1024]{1,0:T(8,128)(2,1)S(1)}, u32[]{:S(2)}, u32[]{:S(2)}) collective-permute-start(bf16[128,1024]{1,0:T(8,128)(2,1)S(1)} %add_convert_fusion), channel_id=1, source_target_pairs={{128,0},{120,248},{129,1},{121,249},{130,2},{122,250},{131,3},{123... | collective-permute-start | bytes 786440 | tf_op jit(solution)/shard_map/ppermute | solution.py:79
Sparse Core Ops, SparseCore 0:
  21.9 71.4 all-gather.1
